TPU v7x, 128 devices: a whole 4x4x4 slice. The times are simulated.
128 devices in a mesh: grp: 2 (over x_lo), dev: 32 (over x_hi, z, y), sub: 2 (over core).
Axes of the slice: x: 4 (x_hi: 2, x_lo: 2; x = x_hi * 2 + x_lo), y: 4, z: 4, core: 2. Of those that a mesh axis runs over, the one named last changes fastest.
Arguments:
- queries: bfloat16 [320, 8192], P(('grp', 'dev'), 'sub'), may hold values from -200 to 200
- new_keys: bfloat16 [320, 512], P(('grp', 'dev'), 'sub'), may hold values from -6 to 6
- new_values: bfloat16 [320, 512], P(('grp', 'dev'), 'sub'), may hold values from -6 to 6
- key_cache: bfloat16 [320, 384, 512], P(('grp', 'dev'), None, 'sub'), may hold values from -6 to 6
- value_cache: bfloat16 [320, 384, 512], P(('grp', 'dev'), None, 'sub'), may hold values from -6 to 6
- lengths: int32 [320], P(('grp', 'dev')), may hold values from 1 to 384, as said below
- residual: bfloat16 [320, 16384], P('grp', ('dev', 'sub')), may hold values from -6 to 6
- o_weight: bfloat16 [8192, 16384], P('sub', 'dev'), may hold values from -0.5 to 0.5
- norm_gain: bfloat16 [16384], P(('dev', 'sub')), may hold values from 0.5 to 1.5
- w_gate: bfloat16 [26624, 16384], P(('grp', 'dev', 'sub')), may hold values from -0.046875 to 0.046875
- w_up: bfloat16 [26624, 16384], P(('grp', 'dev', 'sub')), may hold values from -0.046875 to 0.046875
- w_down: bfloat16 [26624, 16384], P(('grp', 'dev', 'sub')), may hold values from -0.125 to 0.125
Outputs:
- layer_out: bfloat16 [320, 16384], P('grp', ('dev', 'sub'))
Inputs may be any that keep to these rules, and one draw needn't show every extreme that they name: `lengths`: some request uses all 384 positions.
All inputs are finite; a program needn't handle non-finite values.
Results may differ from a plain program's by a relative error of at most 0.015.
Values may be sent and summed in bfloat16 or wider, within the bound.
A program may use at most 128 MiB of HBM per device.

v0:
```python
import jax
import jax.numpy as jnp
from jax import lax
from jax.sharding import PartitionSpec as P

D = 16384
HEAD_DIM = 128


def attend(queries, new_keys, new_values, key_cache, value_cache, lengths):
    row_count = queries.shape[0]
    local_kv = new_keys.shape[1] // HEAD_DIM
    per_group = queries.shape[1] // new_keys.shape[1]
    key_span = key_cache.shape[1]
    rescale_factor = 1.0 / HEAD_DIM**0.5
    query_head_rows = queries.reshape(row_count, local_kv, per_group, HEAD_DIM)
    keys_local = key_cache.reshape(row_count, key_span, local_kv, HEAD_DIM)
    values_local = value_cache.reshape(row_count, key_span, local_kv, HEAD_DIM)
    new_key_shard = new_keys.reshape(row_count, local_kv, HEAD_DIM)
    newv_local = new_values.reshape(row_count, local_kv, HEAD_DIM)
    attention_scores = (
        jnp.einsum(
            "bkgd,blkd->bkgl", query_head_rows, keys_local, preferred_element_type=jnp.float32
        )
        * rescale_factor
    )
    self_key_score = (
        jnp.einsum(
            "uyvz,uyz->uyv", query_head_rows, new_key_shard, preferred_element_type=jnp.float32
        )
        * rescale_factor
    )
    valid = (jnp.arange(key_span, dtype=jnp.int32)[None, :] < lengths[:, None])[:, None, None, :]
    masked = jnp.where(valid, attention_scores, jnp.float32(-1e30))
    top_score = jnp.maximum(jnp.max(masked, axis=3), self_key_score)
    weights = jnp.where(valid, jnp.exp(masked - top_score[..., None]), jnp.float32(0.0))
    own_weight = jnp.exp(self_key_score - top_score)
    total = jnp.sum(weights, axis=3) + own_weight
    probs = (weights / total[..., None]).astype(jnp.bfloat16)
    own_probs = (own_weight / total).astype(jnp.bfloat16)
    context = jnp.einsum("bkgl,blkd->bkgd", probs, values_local, preferred_element_type=jnp.float32)
    context = (
        context
        + own_probs.astype(jnp.float32)[..., None] * newv_local.astype(jnp.float32)[:, :, None, :]
    )
    return context.astype(jnp.bfloat16).reshape(row_count, local_kv * per_group * HEAD_DIM)


def shards(
    queries,
    new_keys,
    new_values,
    key_cache,
    value_cache,
    lengths,
    residual,
    o_weight,
    norm_gain,
    w_gate,
    w_up,
    w_down,
):
    context = attend(queries, new_keys, new_values, key_cache, value_cache, lengths)
    partial_out = jnp.dot(
        lax.all_gather(context, "dev", axis=0, tiled=True),
        o_weight,
        preferred_element_type=jnp.float32,
    )
    attention = lax.psum_scatter(
        partial_out.astype(jnp.bfloat16), "sub", scatter_dimension=1, tiled=True
    ).astype(jnp.float32)
    middle_hidden = residual.astype(jnp.float32) + attention
    squares = lax.psum(jnp.sum(middle_hidden * middle_hidden, axis=1), ("dev", "sub"))
    inverse = lax.rsqrt(squares / D + 1e-05)
    normed = (middle_hidden * inverse[:, None] * norm_gain.astype(jnp.float32)[None, :]).astype(
        jnp.bfloat16
    )
    contract = (((1,), (1,)), ((), ()))
    full_rows = lax.all_gather(normed, ("dev", "sub"), axis=1, tiled=True)
    all_rows = lax.all_gather(full_rows, "grp", axis=0, tiled=True)
    gate_sum = lax.dot_general(all_rows, w_gate, contract, preferred_element_type=jnp.float32)
    up_sum = lax.dot_general(all_rows, w_up, contract, preferred_element_type=jnp.float32)
    hidden = (jax.nn.silu(gate_sum) * up_sum).astype(jnp.bfloat16)
    down_terms = jnp.dot(hidden, w_down, preferred_element_type=jnp.float32)
    by_columns = lax.psum_scatter(down_terms, ("dev", "sub"), scatter_dimension=1, tiled=True)
    feed_out = lax.psum_scatter(
        by_columns.astype(jnp.bfloat16), "grp", scatter_dimension=0, tiled=True
    ).astype(jnp.float32)
    return (middle_hidden + feed_out).astype(jnp.bfloat16)


def solution(mesh):
    placed = (
        P(("grp", "dev"), "sub"),
        P(("grp", "dev"), "sub"),
        P(("grp", "dev"), "sub"),
        P(("grp", "dev"), None, "sub"),
        P(("grp", "dev"), None, "sub"),
        P(("grp", "dev")),
        P("grp", ("dev", "sub")),
        P("sub", "dev"),
        P(("dev", "sub")),
        P(("grp", "dev", "sub"), None),
        P(("grp", "dev", "sub"), None),
        P(("grp", "dev", "sub"), None),
    )
    return jax.shard_map(
        shards, mesh=mesh, in_specs=placed, out_specs=P("grp", ("dev", "sub")), check_vma=False
    )
```

profile of v0, /device:TPU:0, one launch (start us, length us, event | category | flops | bytes accessed | tf_op | source)
XLA Modules:
  0.0 891.9 jit_solution(15343812109811052574)
XLA Ops:
  6.5 0.8 iota_compare_fusion
  7.4 0.7 reshape.57
  8.1 0.7 reshape.50
  8.8 0.8 copy.23
  9.8 0.5 fusion.23
  10.3 0.2 fusion.13
  10.5 1.5 fusion.3
  12.1 0.7 reshape.51
  12.9 73.3 %all-gather.9.cloned.1.call-done = bf16[32,5,4096]{2,1,0:T(8,128)(2,1)} async-done(((bf16[1,5,4096]{2,1,0:T(8,128)(2,1)}), bf16[32,5,4096]{2,1,0:T(8,128)(2,1)}) %all-gather.9.cloned.1.call-update) | async-done | bytes 1310736 | tf_op jit(solution)/shard_map/all_gather | solution.py:65
  86.2 1.8 reshape.52
  88.0 3.7 convolution_convert_fusion
  91.8 8.4 reduce-scatter.4.cloned.1.call-done
  100.2 1.0 multiply_reduce_fusion
  101.2 170.2 %psum.7 = f32[160]{0:T(256)S(1)} all-reduce(f32[160]{0:T(256)S(1)} %multiply_reduce_fusion), channel_id=1, replica_groups=mesh['grp'=2,'dev'=32,'sub'=2] {'dev','sub'}, use_global_device_ids=true, to_apply=%region_4.5 | all-reduce | flops 160 | bytes 1280 | tf_op jit(solution)/shard_map/psum | solution.py:73
  271.4 1.6 multiply_convert_fusion
  273.0 66.2 %all-gather.5.cloned.1.call-done = bf16[160,16384]{1,0:T(8,128)(2,1)} async-done(((bf16[160,256]{1,0:T(8,128)(2,1)}), bf16[160,16384]{1,0:T(8,128)(2,1)}) %all-gather.5.cloned.1.call-update) | async-done | bytes 5242896 | tf_op jit(solution)/shard_map/all_gather | solution.py:79
  339.2 0.2 reduce-scatter.6.cloned.1.call-start
  339.5 132.9 %all-gather.7.cloned.1.call-done = bf16[320,16384]{1,0:T(8,128)(2,1)} async-done(((bf16[160,16384]{1,0:T(8,128)(2,1)}), bf16[320,16384]{1,0:T(8,128)(2,1)}) %all-gather.7.cloned.1.call-update) | async-done | bytes 10485776 | tf_op jit(solution)/shard_map/all_gather | solution.py:80
  472.4 10.1 %fusion.25 = f32[320,208]{0,1:T(8,128)S(1)} fusion(bf16[320,16384]{1,0:T(8,128)(2,1)} %all-gather.7.cloned.1.call-done, bf16[208,16384]{1,0:T(8,128)(2,1)} %param.21), kind=kOutput, calls=%fused_computation.40 | convolution fusion | flops 2181038080 | bytes 17567744 | tf_op jit(solution)/shard_map/dot_general | solution.py:81
  482.5 22.6 %fusion.2 = f32[320,16384]{1,0:T(8,128)} fusion(bf16[208,16384]{1,0:T(8,128)(2,1)} %param.23, bf16[320,16384]{1,0:T(8,128)(2,1)} %all-gather.7.cloned.1.call-done, bf16[208,16384]{1,0:T(8,128)(2,1)} %param.22, f32[320,208]{0,1:T(8,128)S(1)} %fusion.25), kind=kOutput, calls=%fused_computation.5 | convolution fusion | flops 4362475520 | bytes 45355008 | tf_op jit(solution)/shard_map/dot_general | solution.py:84
  505.2 368.5 %reduce-scatter.6.cloned.1.call-done = f32[320,256]{1,0:T(8,128)} async-done(((f32[320,16384]{1,0:T(8,128)}), f32[320,256]{1,0:T(8,128)}) %reduce-scatter.6.cloned.1.call-update) | async-done | bytes 327696 | tf_op jit(solution)/shard_map/reduce_scatter | solution.py:85
  873.7 1.7 convert_element_type.61
  875.4 8.1 reduce-scatter.8.cloned.1.call-done
  883.5 1.6 add_convert_fusion
  (28 shorter events, 0.5 us)
Async XLA Ops:
  6.5 3.2 copy-start
  6.5 85.2 %copy-start.5 = (bf16[256]{0:T(256)(128)(2,1)S(1)}, bf16[256]{0:T(256)(128)(2,1)}, u32[]{:S(2)}) copy-start(bf16[256]{0:T(256)(128)(2,1)} %param.20) | copy-start | bytes 1540
  6.5 93.6 %copy-start.2 = (bf16[160,256]{1,0:T(8,128)(2,1)S(1)}, bf16[160,256]{1,0:T(8,128)(2,1)}, u32[]{:S(2)}) copy-start(bf16[160,256]{1,0:T(8,128)(2,1)} %param.18) | copy-start | bytes 245764
  6.5 79.6 %all-gather.9.cloned.1.call-start = ((), (), s32[]{:S(2)}) async-start(), calls=%async_computation.8 | async-start | bytes 2162688 | tf_op jit(solution)/shard_map/all_gather | solution.py:65
  12.8 87.3 %reduce-scatter.4.cloned.1.call-start = ((), (), s32[]{:S(2)}) async-start(), calls=%async_computation.3 | async-start | bytes 245760 | tf_op jit(solution)/shard_map/reduce_scatter | solution.py:69
  91.7 247.5 %all-gather.5.cloned.1.call-start = ((), (), s32[]{:S(2)}) async-start(), calls=%async_computation.4 | async-start | bytes 5324800 | tf_op jit(solution)/shard_map/all_gather | solution.py:79
  273.0 199.4 %all-gather.7.cloned.1.call-start = ((), (), s32[]{:S(2)}) async-start(), calls=%async_computation.5 | async-start | bytes 15728640 | tf_op jit(solution)/shard_map/all_gather | solution.py:80
  339.2 534.5 %reduce-scatter.6.cloned.1.call-start = ((), (), s32[]{:S(2)}) async-start(), calls=%async_computation.6 | async-start | bytes 21299200 | tf_op jit(solution)/shard_map/reduce_scatter | solution.py:85
  505.1 379.9 %copy-start.1 = (bf16[5,384,256]{2,1,0:T(8,128)(2,1)S(1)}, bf16[5,384,256]{2,1,0:T(8,128)(2,1)}, u32[]{:S(2)}) copy-start(bf16[5,384,256]{2,1,0:T(8,128)(2,1)} %param.15) | copy-start | bytes 2949124
  505.1 378.4 %copy-start.3 = (bf16[160,256]{1,0:T(8,128)(2,1)S(1)}, bf16[160,256]{1,0:T(8,128)(2,1)}, u32[]{:S(2)}) copy-start(bf16[160,256]{1,0:T(8,128)(2,1)} %param.18) | copy-start | bytes 245764
  505.1 378.4 %copy-start.4 = (bf16[160,256]{1,0:T(8,128)(2,1)S(1)}, bf16[160,256]{1,0:T(8,128)(2,1)}, u32[]{:S(2)}) copy-start(bf16[160,256]{1,0:T(8,128)(2,1)} %reduce-scatter.4.cloned.1.call-done) | copy-start | bytes 245764
  505.2 378.3 %reduce-scatter.8.cloned.1.call-start = ((), (), s32[]{:S(2)}) async-start(), calls=%async_computation.7 | async-start | bytes 245760 | tf_op jit(solution)/shard_map/reduce_scatter | solution.py:86
Sparse Core Ops, SparseCore 0:
  12.9 73.1 all-gather.8
  91.8 8.2 reduce-scatter.3
  273.1 66.0 all-gather.4
  340.7 131.5 all-gather.6
  505.3 368.4 reduce-scatter.5
  875.9 7.5 reduce-scatter.7
where the time goes:
time: 893 us; the launch traced here: 892 us
  waiting for transfers between devices  657 us (74%)
  blocking collectives  170 us (19%)
  matrix products  38.6 us (4%)
  between operations  13.5 us (2%)
    reduce_scatter x1, waiting for transfers between devices, shards(): lax.psum_scatter(down_terms, ('dev', 'sub'), scatter_dimension=1, tiled=T...  369 us
    psum x1, blocking collectives, shards(): lax.psum(jnp.sum(middle_hidden * middle_hidden, axis=1), ('dev', 'sub'))  170 us
    all_gather x1, waiting for transfers between devices, shards(): all_rows = lax.all_gather(full_rows, 'grp', axis=0, tiled=True)  133 us
    all_gather x1, waiting for transfers between devices, shards(): lax.all_gather(context, 'dev', axis=0, tiled=True)  73.3 us
    all_gather x1, waiting for transfers between devices, shards(): full_rows = lax.all_gather(normed, ('dev', 'sub'), axis=1, tiled=True)  66.2 us
    dot_general x1, matrix products, shards(): down_terms = jnp.dot(hidden, w_down, preferred_element_type=jnp.float32)  22.6 us
  transfers between devices with their start and end apart: 6, of which 6 were waited for; matrix products, arithmetic and copies ran while one was open for 0% of the time, Pallas kernels for 0%

commit v1 on v0

--- a/solution.py
+++ b/solution.py
@@ -1,10 +1,391 @@
+import functools
+
 import jax
 import jax.numpy as jnp
 from jax import lax
+from jax.experimental import pallas as pl
+from jax.experimental.pallas import tpu as pltpu
 from jax.sharding import PartitionSpec as P
 
 D = 16384
 HEAD_DIM = 128
+MESH = pl.DeviceIdType.MESH
+F32, BF16 = jnp.float32, jnp.bfloat16
+ROWS, HID = 160, 208
+CHUNKS = {"0": (0, 0), "1": (slice(1, 4), 0), "2": (0, slice(1, 4)), "3": (slice(1, 4), slice(1, 4))}
+PARTS = (
+    ((0, 1, 2), 0, (0, 112), ((0, (0, 64)), (0, (64, 112)))),
+    ((1, 2, 0), 1, (0, 112), ((1, (0, 64)), (1, (64, 112)))),
+    ((2, 0, 1), slice(0, 2), (112, 160), ((0, (112, 160)), (1, (112, 160)))),
+)
+
+
+def place():
+    grp, dev, sub = lax.axis_index("grp"), lax.axis_index("dev"), lax.axis_index("sub")
+    return [(dev // 16) * 2 + grp, dev % 4, (dev // 4) % 4], sub
+
+
+def device(at, sub):
+    x, y, z = at
+    return (lax.rem(x, 2), (x // 2) * 16 + z * 4 + y, sub)
+
+
+def shifted(at, dim, by):
+    at = list(at)
+    at[dim] = lax.rem(at[dim] + by, 4)
+    return at
+
+
+class Wires:
+    def __init__(self, at, sub, send, recv):
+        self.at, self.sub, self.send, self.recv, self.n = at, sub, send, recv, 0
+        self.started = []
+
+    def post(self, src, dst, dim, by):
+        if dim is None:
+            to = device(self.at, 1 - self.sub)
+        else:
+            to = device(shifted(self.at, dim, by), self.sub)
+        copy = pltpu.make_async_remote_copy(
+            src_ref=src, dst_ref=dst, send_sem=self.send.at[self.n], recv_sem=self.recv.at[self.n],
+            device_id=to, device_id_type=MESH,
+        )
+        copy.start()
+        self.n += 1
+        self.started.append(copy)
+        return copy
+
+    def drain(self):
+        for copy in self.started:
+            copy.wait_send()
+        self.started = []
+
+
+def block(buf, part, a, b, c, tail=(), half=None):
+    dims, h, rows, halves = PARTS[part]
+    if half is not None:
+        h, rows = halves[half]
+    idx = [None] * 3
+    idx[dims[0]], idx[dims[1]], idx[dims[2]] = a, b, c
+    return buf.at[tuple(idx) + tuple(tail) + (h, slice(*rows), slice(None))]
+
+
+def lay(part, a, b):
+    return (b, a) if part == 2 else (a, b)
+
+
+def flat(buf, part, lead, half=None):
+    _, h, rows, halves = PARTS[part]
+    if half is not None:
+        h, rows = halves[half]
+    return buf.at[tuple(lead) + (h, slice(*rows), slice(None))]
+
+
+def gather(w, XB, sq, ready):
+    m1, m2a, m2b, m3, fwd = {}, {}, {}, {}, {}
+    own = lambda p: block(XB, p, 0, 0, 0, (0,))
+    xb = lambda p, a, b, c, half=None, s=0: block(XB, p, a, b, c, (s,), half)
+    d2d = []
+
+    def plane(p, c, up=True):
+        a, b = CHUNKS[c]
+        d3 = PARTS[p][0][2]
+        m3[p, c] = [
+            w.post(xb(p, a, b, 0), xb(p, a, b, 3), d3, 1),
+            w.post(xb(p, a, b, 0), xb(p, a, b, 1), d3, 3),
+        ]
+
+    def onward(p, c):
+        a, b = CHUNKS[c]
+        d3 = PARTS[p][0][2]
+        for copy in m3[p, c]:
+            copy.wait_recv()
+        fwd[p, c] = [
+            w.post(xb(p, a, b, 3, 0), xb(p, a, b, 2, 0), d3, 1),
+            w.post(xb(p, a, b, 1, 1), xb(p, a, b, 2, 1), d3, 3),
+        ]
+
+    def across(p, a, b, c):
+        d2d.append(w.post(xb(p, a, b, c), xb(p, a, b, c, s=1), None, 0))
+
+    for p in range(3):
+        d1 = PARTS[p][0][0]
+        m1[p] = [w.post(own(p), xb(p, 4 - k, 0, 0), d1, k) for k in (1, 3, 2)]
+    for p in range(3):
+        d2 = PARTS[p][0][1]
+        m2a[p] = [w.post(own(p), xb(p, 0, 4 - k, 0), d2, k) for k in (1, 3, 2)]
+    for p in range(3):
+        plane(p, "0")
+    sq(0)
+    for p in range(3):
+        d2 = PARTS[p][0][1]
+        for copy in m1[p]:
+            copy.wait_recv()
+        m2b[p] = [w.post(xb(p, slice(1, 4), 0, 0), xb(p, slice(1, 4), 4 - k, 0), d2, k) for k in (1, 3, 2)]
+        plane(p, "1")
+        across(p, slice(0, 4), 0, 0)
+    for p in range(3):
+        for copy in m2a[p]:
+            copy.wait_recv()
+        plane(p, "2")
+    sq(1)
+    for p in range(3):
+        onward(p, "0")
+    for p in range(3):
+        for copy in m2b[p]:
+            copy.wait_recv()
+        plane(p, "3")
+        across(p, slice(0, 4), slice(1, 4), 0)
+    sq(2)
+    for p in range(3):
+        onward(p, "1")
+    for p in range(3):
+        onward(p, "2")
+    sq(3)
+    ready(0)
+    for p in range(3):
+        onward(p, "3")
+        across(p, slice(0, 4), slice(0, 4), 1)
+        across(p, slice(0, 4), slice(0, 4), 3)
+    sq(4)
+    ready(1)
+    for p in range(3):
+        for c in "0123":
+            for copy in fwd[p, c]:
+                copy.wait_recv()
+        across(p, slice(0, 4), slice(0, 4), 2)
+    for copy in d2d:
+        copy.wait_recv()
+    ready(2)
+
+
+def ffn_kernel(mid_ref, gain_ref, wg_hbm, wu_hbm, wd_hbm, out_ref,
+               XB, PB, SB, RB, FB, G1, G3, HB, JB, sqs, sqr, wg, wu, wd, acc, hid, wsem, send, recv):
+    at, sub = place()
+    x0, y0, z0 = at
+    grp = lax.rem(x0, 2)
+    w = Wires(at, sub, send, recv)
+    loads = [pltpu.make_async_copy(a, b, wsem.at[i]) for i, (a, b) in enumerate(((wg_hbm, wg), (wu_hbm, wu), (wd_hbm, wd)))]
+    for load in loads:
+        load.start()
+    barrier = pltpu.get_barrier_semaphore()
+    for dim in range(3):
+        for by in (1, 2, 3):
+            pl.semaphore_signal(barrier, inc=1, device_id=device(shifted(at, dim, by), sub), device_id_type=MESH)
+    pl.semaphore_signal(barrier, inc=1, device_id=device(at, 1 - sub), device_id_type=MESH)
+
+    mid = mid_ref[...]
+    rows = (mid * gain_ref[...].astype(F32)).astype(BF16)
+    XB[0, 0, 0, 0, 0] = rows[:, :128]
+    XB[0, 0, 0, 0, 1] = rows[:, 128:]
+    eye = lax.broadcasted_iota(jnp.int32, (ROWS, 256), 0) == lax.broadcasted_iota(jnp.int32, (ROWS, 256), 1)
+    column = jnp.sum(mid * mid, axis=1, keepdims=True)
+    sqs[0] = jnp.broadcast_to(jnp.sum(jnp.where(eye, column, 0.0), axis=0, keepdims=True), (8, 256))
+    pl.semaphore_wait(barrier, 10)
+
+    sq_copies = {}
+
+    def sq(step):
+        if step > 0:
+            total = sqs[step - 1]
+            for i, copy in enumerate(sq_copies[step - 1]):
+                copy.wait_recv()
+                total = total + sqr[(step - 1) * 3 + i]
+            sqs[step] = total
+        if step == 0:
+            sq_copies[0] = [w.post(sqs.at[0], sqr.at[0], None, 0)]
+        elif step == 1:
+            sq_copies[1] = [w.post(sqs.at[1], sqr.at[3 + i], 1, k) for i, k in enumerate((1, 3, 2))]
+        elif step == 2:
+            sq_copies[2] = [w.post(sqs.at[2], sqr.at[6 + i], 2, k) for i, k in enumerate((1, 3, 2))]
+        elif step == 3:
+            sq_copies[3] = [w.post(sqs.at[3], sqr.at[9], 0, 2)]
+        else:
+            sq_copies[4] = [w.post(sqs.at[4], sqr.at[12], 0, 1)]
+
+    def dev_at(rx, ry, rz):
+        return (lax.rem(x0 + rx, 4) // 2) * 16 + lax.rem(z0 + rz, 4) * 4 + lax.rem(y0 + ry, 4)
+
+    def ready(step):
+        if step != 2:
+            return
+        loads[0].wait()
+        loads[1].wait()
+        acc[...] = jnp.zeros_like(acc)
+
+        @pl.loop(0, 32)
+        def _(i):
+            rx, ry, rz = (i // 16) * 2, (i // 4) % 4, i % 4
+            other = lax.rem(rx + 5 - 2 * grp, 4)
+            k = pl.multiple_of(dev_at(rx, ry, rz) * 512, 512)
+            lhs = jnp.concatenate(
+                [
+                    jnp.concatenate([XB[q, ry, rz, s, h] for s in (sub, 1 - sub) for h in (0, 1)], axis=1)
+                    for q in (rx, other)
+                ],
+                axis=0,
+            )
+            for j, weight in enumerate((wg, wu)):
+                acc[j] += lax.dot_general(
+                    lhs, weight[:, pl.ds(k, 512)], (((1,), (1,)), ((), ())), preferred_element_type=F32
+                )
+
+    gather(w, XB, sq, ready)
+
+    sq_copies[4][0].wait_recv()
+    for i, sums in enumerate((sqs[4], sqr[12])):
+        inv_row = lax.rsqrt(sums[0:1] / D + 1e-05)
+        inv = jnp.sum(jnp.where(eye, inv_row, 0.0), axis=1, keepdims=True)
+        gate = acc[0, i * ROWS:(i + 1) * ROWS] * inv
+        up = acc[1, i * ROWS:(i + 1) * ROWS] * inv
+        hid[i] = (gate / (1.0 + jnp.exp(-gate)) * up).astype(BF16)
+    loads[2].wait()
+    scatter(w, dev_at, sub, hid, wd, PB, SB, RB, FB, G1, G3, HB, JB)
+    out_ref[...] = (mid_ref[...] + jnp.concatenate([PB[0, 0, 0, 0], PB[0, 0, 0, 1]], axis=1).astype(F32)).astype(BF16)
+    w.drain()
+
+
+def scatter(w, dev_at, sub, hid, wd, PB, SB, RB, FB, G1, G3, HB, JB):
+    def blocks(p, c3, target, core, extra):
+        dims, h, (r0, r1), _ = PARTS[p]
+
+        @pl.loop(0, 16)
+        def _(i):
+            r = [None] * 3
+            r[dims[0]], r[dims[1]], r[dims[2]] = i // 4, i % 4, c3
+            rx, ry, rz = r
+            lhs = hid[lax.rem(rx, 2), r0:r1]
+            col = dev_at(rx, ry, rz) * 512 + core * 256
+            for hh in (0, 1) if p == 2 else (h,):
+                part = jnp.dot(lhs, wd[:, pl.ds(pl.multiple_of(col + hh * 128, 128), 128)], preferred_element_type=F32)
+                if extra is not None:
+                    part = part + extra[rx, ry, rz, hh, r0:r1].astype(F32)
+                target[rx, ry, rz, hh, r0:r1] = part.astype(BF16)
+
+    def add(target, sources, p, count, where, half=None):
+        _, h, (r0, r1), halves = PARTS[p]
+        if half is not None:
+            h, (r0, r1) = halves[half]
+        hs = (0, 1) if isinstance(h, slice) else (h,)
+
+        def one(i):
+            t, ss = where(i)
+            for hh in hs:
+                total = target[tuple(t) + (hh, slice(r0, r1))].astype(F32)
+                for source, s in zip(sources, ss):
+                    total = total + source[tuple(s) + (hh, slice(r0, r1))].astype(F32)
+                target[tuple(t) + (hh, slice(r0, r1))] = total.astype(BF16)
+
+        if count == 1:
+            one(0)
+        else:
+            pl.loop(0, count)(one)
+
+    def cell(c, i):
+        return {"0": (0, 0), "1": (i + 1, 0), "2": (0, i + 1), "3": (i // 3 + 1, i % 3 + 1)}[c]
+
+    count = {"0": 1, "1": 3, "2": 3, "3": 9}
+
+    def spot(p, a, b, c):
+        dims = PARTS[p][0]
+        r = [None] * 3
+        r[dims[0]], r[dims[1]], r[dims[2]] = a, b, c
+        return tuple(r)
+
+    order = (2, 1, 3, 0)
+    full = slice(0, 4)
+    swap = {}
+    for c3 in order:
+        for p in range(3):
+            blocks(p, c3, SB, 1 - sub, None)
+            swap[p, c3] = w.post(block(SB, p, full, full, c3), block(RB, p, full, full, c3), None, 0)
+    first, second = {}, {}
+    for c3 in order:
+        for p in range(3):
+            d3 = PARTS[p][0][2]
+            swap[p, c3].wait_recv()
+            blocks(p, c3, PB, sub, RB)
+            if c3 == 2:
+                for c in "3210":
+                    a, b = CHUNKS[c]
+                    first[p, c] = [
+                        w.post(block(PB, p, a, b, 2, half=0), flat(FB, p, lay(p, a, b), 0), d3, 1),
+                        w.post(block(PB, p, a, b, 2, half=1), flat(FB, p, lay(p, a, b), 1), d3, 3),
+                    ]
+    for c in "3210":
+        a, b = CHUNKS[c]
+        for p in range(3):
+            d3 = PARTS[p][0][2]
+            for q, c3 in ((0, 1), (1, 3)):
+                first[p, c][q].wait_recv()
+                add(PB, (FB,), p, count[c], lambda i: (spot(p, *cell(c, i), c3), (lay(p, *cell(c, i)),)), half=q)
+            second[p, c] = [
+                w.post(block(PB, p, a, b, 1), flat(G1, p, lay(p, a, b)), d3, 1),
+                w.post(block(PB, p, a, b, 3), flat(G3, p, lay(p, a, b)), d3, 3),
+            ]
+    third, fourth = {}, {}
+    for c in "3210":
+        for p in range(3):
+            d2 = PARTS[p][0][1]
+            for copy in second[p, c]:
+                copy.wait_recv()
+            add(PB, (G1, G3), p, count[c], lambda i: (spot(p, *cell(c, i), 0), (lay(p, *cell(c, i)),) * 2))
+            if c in "32":
+                a = CHUNKS[c][0]
+                third[p, c] = [
+                    w.post(block(PB, p, a, k, 0), flat(HB, p, (k - 1, a)), d2, k) for k in (1, 3, 2)
+                ]
+    for c, a in (("3", slice(1, 4)), ("2", 0)):
+        for p in range(3):
+            d1 = PARTS[p][0][0]
+            for copy in third[p, c]:
+                copy.wait_recv()
+            n, base = (3, 1) if c == "3" else (1, 0)
+            add(PB, (HB,) * 3, p, n, lambda i: (spot(p, i + base, 0, 0), tuple((k, i + base) for k in range(3))))
+            if c == "3":
+                fourth[p] = [w.post(block(PB, p, k, 0, 0), flat(JB, p, (k - 1,)), d1, k) for k in (1, 3, 2)]
+    for p in range(3):
+        for copy in fourth[p]:
+            copy.wait_recv()
+        add(PB, (JB,) * 3, p, 1, lambda i: (spot(p, 0, 0, 0), tuple((k,) for k in range(3))))
+
+
+def ffn(mid, gain, wg, wu, wd):
+    hbm = pl.BlockSpec(memory_space=pl.ANY)
+    vmem = pl.BlockSpec(memory_space=pltpu.VMEM)
+    grid = (4, 4, 4)
+    tail = (2, ROWS, 128)
+    return pl.pallas_call(
+        ffn_kernel,
+        out_shape=jax.ShapeDtypeStruct((ROWS, 256), BF16),
+        in_specs=[vmem, vmem, hbm, hbm, hbm],
+        out_specs=vmem,
+        scratch_shapes=[
+            pltpu.VMEM(grid + (2,) + tail, BF16),
+            pltpu.VMEM(grid + tail, BF16),
+            pltpu.VMEM(grid + tail, BF16),
+            pltpu.VMEM(grid + tail, BF16),
+            pltpu.VMEM((4, 4) + tail, BF16),
+            pltpu.VMEM((4, 4) + tail, BF16),
+            pltpu.VMEM((4, 4) + tail, BF16),
+            pltpu.VMEM((3, 4) + tail, BF16),
+            pltpu.VMEM((3,) + tail, BF16),
+            pltpu.VMEM((5, 8, 256), F32),
+            pltpu.VMEM((13, 8, 256), F32),
+            pltpu.VMEM((HID, D), BF16),
+            pltpu.VMEM((HID, D), BF16),
+            pltpu.VMEM((HID, D), BF16),
+            pltpu.VMEM((2, 2 * ROWS, HID), F32),
+            pltpu.VMEM((2, ROWS, HID), BF16),
+            pltpu.SemaphoreType.DMA((3,)),
+            pltpu.SemaphoreType.DMA((200,)),
+            pltpu.SemaphoreType.DMA((200,)),
+        ],
+        compiler_params=pltpu.CompilerParams(
+            collective_id=1, has_side_effects=True, vmem_limit_bytes=60 * 2**20
+        ),
+        name="ffn",
+    )(mid, gain, wg, wu, wd)
 
 
 def attend(queries, new_keys, new_values, key_cache, value_cache, lengths):
@@ -70,23 +451,7 @@
         partial_out.astype(jnp.bfloat16), "sub", scatter_dimension=1, tiled=True
     ).astype(jnp.float32)
     middle_hidden = residual.astype(jnp.float32) + attention
-    squares = lax.psum(jnp.sum(middle_hidden * middle_hidden, axis=1), ("dev", "sub"))
-    inverse = lax.rsqrt(squares / D + 1e-05)
-    normed = (middle_hidden * inverse[:, None] * norm_gain.astype(jnp.float32)[None, :]).astype(
-        jnp.bfloat16
-    )
-    contract = (((1,), (1,)), ((), ()))
-    full_rows = lax.all_gather(normed, ("dev", "sub"), axis=1, tiled=True)
-    all_rows = lax.all_gather(full_rows, "grp", axis=0, tiled=True)
-    gate_sum = lax.dot_general(all_rows, w_gate, contract, preferred_element_type=jnp.float32)
-    up_sum = lax.dot_general(all_rows, w_up, contract, preferred_element_type=jnp.float32)
-    hidden = (jax.nn.silu(gate_sum) * up_sum).astype(jnp.bfloat16)
-    down_terms = jnp.dot(hidden, w_down, preferred_element_type=jnp.float32)
-    by_columns = lax.psum_scatter(down_terms, ("dev", "sub"), scatter_dimension=1, tiled=True)
-    feed_out = lax.psum_scatter(
-        by_columns.astype(jnp.bfloat16), "grp", scatter_dimension=0, tiled=True
-    ).astype(jnp.float32)
-    return (middle_hidden + feed_out).astype(jnp.bfloat16)
+    return ffn(middle_hidden, norm_gain[None, :], w_gate, w_up, w_down)
 
 
 def solution(mesh):

time: 893 us -> 247 us (0.28)
  waiting for transfers between devices: 657 us -> 81.2 us
  blocking collectives: 170 us -> 0 us
  Pallas kernels: 0 us -> 134 us
  matrix products: 38.6 us -> 5.9 us
    reduce_scatter x2 -> x0, waiting for transfers between devices: 377 us -> none  [the longest x1 369 us: shards(): lax.psum_scatter(down_terms, ('dev', 'sub'), scatter_dimension=1, tiled=T...]
    all_gather x2 -> x0, waiting for transfers between devices: 199 us -> none  [the longest x1 133 us: shards(): all_rows = lax.all_gather(full_rows, 'grp', axis=0, tiled=True)]
    psum x1 -> x0, blocking collectives: 170 us -> none  [shards(): lax.psum(jnp.sum(middle_hidden * middle_hidden, axis=1), ('dev', 'sub'))]
    pallas_call x0 -> x1, Pallas kernels: none -> 134 us  [ffn(): pl.pallas_call(ffn_kernel, out_shape=jax.ShapeDtypeStruct((ROWS, 256), BF...]
    dot_general x2 -> x0, matrix products: 32.7 us -> none  [the longest x1 22.6 us: shards(): down_terms = jnp.dot(hidden, w_down, preferred_element_type=jnp.float32)]
  transfers between devices with their start and end apart: 6 -> 2, of which waited for: 6 -> 2; matrix products, arithmetic and copies ran while one was open for 0% -> 0% of each run, Pallas kernels for 0% -> 0%
where the time goes in v1:
time: 247 us; the launch traced here: 245 us
  Pallas kernels  134 us (54%)
  waiting for transfers between devices  81.2 us (33%)
  between operations  13.5 us (5%)
  local copies, waits for them, and re-layouts  6.9 us (3%)
  matrix products  5.9 us (2%)
  other arithmetic  2.61 us (1%)
    pallas_call x1, Pallas kernels, ffn(): pl.pallas_call(ffn_kernel, out_shape=jax.ShapeDtypeStruct((ROWS, 256), BF...  134 us
    all_gather x1, waiting for transfers between devices, shards(): lax.all_gather(context, 'dev', axis=0, tiled=True)  73.3 us
    reduce_scatter x1, waiting for transfers between devices, shards(): lax.psum_scatter(partial_out.astype(jnp.bfloat16), 'sub', scatter_dimensi...  7.86 us
  transfers between devices with their start and end apart: 2, of which 2 were waited for; matrix products, arithmetic and copies ran while one was open for 0% of the time, Pallas kernels for 0%

profile of v1, /device:TPU:0, one launch (start us, length us, event | category | flops | bytes accessed | tf_op | source)
XLA Modules:
  0.0 244.5 jit_solution(8456282304470135102)
XLA Ops:
  6.5 0.0 copy-start
  6.5 0.0 all-gather.3.cloned.1.call-start
  6.5 0.8 iota_compare_fusion
  7.4 0.8 copy.23
  8.2 0.7 reshape.55
  8.9 0.1 fusion.15
  9.0 0.5 fusion.14
  9.6 0.2 fusion.6
  9.8 0.7 reshape.48
  10.5 1.5 fusion.1
  12.1 0.7 reshape.49
  12.8 0.0 all-gather.3.cloned.1.call-update
  12.8 0.0 copy-start.2
  12.8 0.0 copy-start.1
  12.8 0.0 reduce-scatter.2.cloned.1.call-start
  12.9 73.3 %all-gather.3.cloned.1.call-done = bf16[32,5,4096]{2,1,0:T(8,128)(2,1)} async-done(((bf16[1,5,4096]{2,1,0:T(8,128)(2,1)}), bf16[32,5,4096]{2,1,0:T(8,128)(2,1)}) %all-gather.3.cloned.1.call-update) | async-done | bytes 1310736 | tf_op jit(solution)/shard_map/all_gather | solution.py:446
  86.1 1.8 reshape.50
  88.0 3.7 %convolution_convert_fusion = bf16[160,512]{1,0:T(8,128)(2,1)} fusion(bf16[160,4096]{1,0:T(8,128)(2,1)S(1)} %reshape.50, bf16[4096,512]{1,0:T(8,128)(2,1)} %param.19), kind=kOutput, calls=%fused_computation | convolution fusion | flops 671170560 | bytes 5668864 | tf_op jit(solution)/shard_map/dot_general | solution.py:445
  91.7 0.0 reduce-scatter.2.cloned.1.call-update
  91.7 0.6 broadcast_in_dim.31.gain_ref
  92.3 7.9 %reduce-scatter.2.cloned.1.call-done = bf16[160,256]{1,0:T(8,128)(2,1)} async-done(((bf16[160,512]{1,0:T(8,128)(2,1)}), bf16[160,256]{1,0:T(8,128)(2,1)}) %reduce-scatter.2.cloned.1.call-update) | async-done | bytes 81936 | tf_op jit(solution)/shard_map/reduce_scatter | solution.py:450
  100.1 1.6 convert_add_fusion.mid_ref
  101.7 134.4 %ffn.1 = bf16[160,256]{1,0:T(8,128)(2,1)} custom-call(f32[160,256]{1,0:T(8,128)} %convert_add_fusion.mid_ref, bf16[1,256]{1,0:T(2,128)(2,1)} %broadcast_in_dim.31.gain_ref, bf16[208,16384]{1,0:T(8,128)(2,1)} %wg_hbm.1, bf16[208,16384]{1,0:T(8,128)(2,1)} %wu_hbm.1, bf16[208,16384]{1,0:T(8,128)(2,1)} %wd_hbm.1), custom_call_target="tpu_custom_call" | custom-call | tf_op jit(solution)/shard_map/ffn/pallas_call | solution.py:358
  236.2 1.5 copy.35
  (5 shorter events, 0.0 us)
Async XLA Ops:
  6.5 2.5 %copy-start = (bf16[5,384,256]{2,1,0:T(8,128)(2,1)S(1)}, bf16[5,384,256]{2,1,0:T(8,128)(2,1)}, u32[]{:S(2)}) copy-start(bf16[5,384,256]{2,1,0:T(8,128)(2,1)} %param.15) | copy-start | bytes 2949124
  6.5 79.6 %all-gather.3.cloned.1.call-start = ((), (), s32[]{:S(2)}) async-start(), calls=%async_computation.2 | async-start | bytes 2162688 | tf_op jit(solution)/shard_map/all_gather | solution.py:446
  12.8 78.9 %copy-start.2 = (bf16[256]{0:T(256)(128)(2,1)S(1)}, bf16[256]{0:T(256)(128)(2,1)}, u32[]{:S(2)}) copy-start(bf16[256]{0:T(256)(128)(2,1)} %param.20) | copy-start | bytes 1540
  12.8 87.3 %copy-start.1 = (bf16[160,256]{1,0:T(8,128)(2,1)S(1)}, bf16[160,256]{1,0:T(8,128)(2,1)}, u32[]{:S(2)}) copy-start(bf16[160,256]{1,0:T(8,128)(2,1)} %param.18) | copy-start | bytes 245764
  12.8 87.3 %reduce-scatter.2.cloned.1.call-start = ((), (), s32[]{:S(2)}) async-start(), calls=%async_computation.1 | async-start | bytes 245760 | tf_op jit(solution)/shard_map/reduce_scatter | solution.py:450
Sparse Core Ops, SparseCore 0:
  12.9 73.1 all-gather.2
  91.8 8.2 reduce-scatter.1

commit v2 on v1

v2 whole, which is shorter than its diff:
```python
import functools

import jax
import jax.numpy as jnp
from jax import lax
from jax.experimental import pallas as pl
from jax.experimental.pallas import tpu as pltpu
from jax.sharding import PartitionSpec as P

D = 16384
HEAD_DIM = 128
MESH = pl.DeviceIdType.MESH
F32, BF16 = jnp.float32, jnp.bfloat16
ROWS, HID, CACHE = 160, 208, 384
CHUNKS = {
    "0": (0, 0), "1": (slice(1, 4), 0), "2": (0, slice(1, 4)),
    "3": (slice(1, 4), 1), "4": (slice(1, 4), 2), "5": (slice(1, 4), 3),
}
PARTS = (
    ((0, 1, 2), 0, (0, 112), ((0, (0, 64)), (0, (64, 112)))),
    ((1, 2, 0), 1, (0, 112), ((1, (0, 64)), (1, (64, 112)))),
    ((2, 0, 1), slice(0, 2), (112, 160), ((0, (112, 160)), (1, (112, 160)))),
)


def place():
    grp, dev, sub = lax.axis_index("grp"), lax.axis_index("dev"), lax.axis_index("sub")
    return [(dev // 16) * 2 + grp, dev % 4, (dev // 4) % 4], sub


def device(at, sub):
    x, y, z = at
    return (lax.rem(x, 2), (x // 2) * 16 + z * 4 + y, sub)


def shifted(at, dim, by):
    at = list(at)
    at[dim] = lax.rem(at[dim] + by, 4)
    return at


class Wires:
    def __init__(self, at, sub, send, recv):
        self.at, self.sub, self.send, self.recv, self.n = at, sub, send, recv, 0
        self.started = []

    def post(self, src, dst, dim, by):
        if dim is None:
            to = device(self.at, 1 - self.sub)
        else:
            to = device(shifted(self.at, dim, by), self.sub)
        copy = pltpu.make_async_remote_copy(
            src_ref=src, dst_ref=dst, send_sem=self.send.at[self.n], recv_sem=self.recv.at[self.n],
            device_id=to, device_id_type=MESH,
        )
        copy.start()
        self.n += 1
        self.started.append(copy)
        return copy

    def drain(self):
        for copy in self.started:
            copy.wait_send()
        self.started = []


def block(buf, part, a, b, c, tail=(), half=None):
    dims, h, rows, halves = PARTS[part]
    if half is not None:
        h, rows = halves[half]
    idx = [None] * 3
    idx[dims[0]], idx[dims[1]], idx[dims[2]] = a, b, c
    return buf.at[tuple(idx) + tuple(tail) + (h, slice(*rows), slice(None))]


def lay(part, a, b):
    return (b, a) if part == 2 else (a, b)


def flat(buf, part, lead, half=None):
    _, h, rows, halves = PARTS[part]
    if half is not None:
        h, rows = halves[half]
    return buf.at[tuple(lead) + (h, slice(*rows), slice(None))]


def gather(w, XB, sq, ready):
    m1, m2a, m2b, m3, fwd = {}, {}, {}, {}, {}
    own = lambda p: block(XB, p, 0, 0, 0, (0,))
    xb = lambda p, a, b, c, half=None, s=0: block(XB, p, a, b, c, (s,), half)
    d2d = []

    def plane(p, c, up=True):
        a, b = CHUNKS[c]
        d3 = PARTS[p][0][2]
        m3[p, c] = [
            w.post(xb(p, a, b, 0), xb(p, a, b, 3), d3, 1),
            w.post(xb(p, a, b, 0), xb(p, a, b, 1), d3, 3),
        ]

    def onward(p, c):
        a, b = CHUNKS[c]
        d3 = PARTS[p][0][2]
        for copy in m3[p, c]:
            copy.wait_recv()
        fwd[p, c] = [
            w.post(xb(p, a, b, 3, 0), xb(p, a, b, 2, 0), d3, 1),
            w.post(xb(p, a, b, 1, 1), xb(p, a, b, 2, 1), d3, 3),
        ]

    def across(p, a, b, c):
        d2d.append(w.post(xb(p, a, b, c), xb(p, a, b, c, s=1), None, 0))

    for p in range(3):
        d1 = PARTS[p][0][0]
        m1[p] = [w.post(own(p), xb(p, 4 - k, 0, 0), d1, k) for k in (1, 3, 2)]
    for p in range(3):
        d2 = PARTS[p][0][1]
        m2a[p] = [w.post(own(p), xb(p, 0, 4 - k, 0), d2, k) for k in (1, 3, 2)]
    for p in range(3):
        plane(p, "0")
    sq(0)
    for p in range(3):
        d2 = PARTS[p][0][1]
        for copy in m1[p]:
            copy.wait_recv()
        m2b[p] = [w.post(xb(p, slice(1, 4), 0, 0), xb(p, slice(1, 4), 4 - k, 0), d2, k) for k in (1, 3, 2)]
        plane(p, "1")
        across(p, slice(0, 4), 0, 0)
    for p in range(3):
        for copy in m2a[p]:
            copy.wait_recv()
        plane(p, "2")
    sq(1)
    for p in range(3):
        onward(p, "0")
    for i, c in enumerate("534"):
        for p in range(3):
            m2b[p][i].wait_recv()
            plane(p, c)
        if i == 0:
            for p in range(3):
                onward(p, "1")
    sq(2)
    for p in range(3):
        across(p, slice(0, 4), slice(1, 4), 0)
        onward(p, "2")
    ready(0)
    sq(3)
    for c in "534":
        for p in range(3):
            onward(p, c)
    for p in range(3):
        across(p, slice(0, 4), slice(0, 4), 1)
        across(p, slice(0, 4), slice(0, 4), 3)
    sq(4)
    ready(1)
    for chunks, r2 in (("01", 0), ("25", 3), ("3", 1), ("4", 2)):
        for p in range(3):
            for c in chunks:
                for copy in fwd[p, c]:
                    copy.wait_recv()
            across(p, slice(0, 4), r2, 2)
    for copy in d2d:
        copy.wait_recv()
    ready(2)


def attention(q_ref, nk_ref, nv_ref, kc, vc, len_ref, qs, CB):
    for h in range(32):
        qs[pl.ds(h, 5, stride=32), :] = q_ref[:, h * 128:(h + 1) * 128].astype(F32)
    span = lax.broadcasted_iota(jnp.int32, (16, CACHE), 1)
    scale = 1.0 / HEAD_DIM**0.5
    for b in range(5):
        for g in range(2):
            cols = slice(g * 128, (g + 1) * 128)
            q = qs[b * 32 + g * 16:b * 32 + (g + 1) * 16]
            scores = lax.dot_general(
                q.astype(BF16), kc[b, :, cols], (((1,), (1,)), ((), ())), preferred_element_type=F32
            ) * scale
            own = jnp.sum(q * nk_ref[b:b + 1, cols].astype(F32), axis=1, keepdims=True) * scale
            valid = span < len_ref[b]
            masked = jnp.where(valid, scores, -1e30)
            top = jnp.maximum(jnp.max(masked, axis=1, keepdims=True), own)
            weights = jnp.where(valid, jnp.exp(masked - top), 0.0)
            own = jnp.exp(own - top)
            total = jnp.sum(weights, axis=1, keepdims=True) + own
            probs = (weights / total).astype(BF16)
            own = (own / total).astype(BF16).astype(F32)
            context = jnp.dot(probs, vc[b, :, cols], preferred_element_type=F32)
            context = context + own * nv_ref[b:b + 1, cols].astype(F32)
            CB[0, 0, 0, b * 32 + g * 16:b * 32 + (g + 1) * 16] = context.astype(BF16)


def project(w, at, sub, CB, LH, wo, wo_load, half_out, half_in):
    x0, y0, z0 = at

    def part(q, rx, ry, rz):
        return CB.at[rx, ry, rz, q * 80:(q + 1) * 80]

    def cut(q, rx, a, b):
        return part(q, rx, *((b, a) if q == 0 else (a, b)))

    dims = ((2, 1), (1, 2))
    turns = (1, 3, 2)
    both = slice(0, 2)

    def settle(rx, ry, rz):
        dev = (lax.rem(x0 + 2 * rx, 4) // 2) * 16 + lax.rem(z0 + rz, 4) * 4 + lax.rem(y0 + ry, 4)
        for b in range(5):
            LH[pl.ds(dev * 5 + b, 32, stride=ROWS), :] = CB[rx, ry, rz, b * 32:(b + 1) * 32].astype(F32)

    hop = [w.post(part(q, 0, 0, 0), part(q, 1, 0, 0), 0, 2) for q in range(2)]
    near = [[w.post(cut(q, 0, 0, 0), cut(q, 0, 4 - k, 0), dims[q][0], k) for k in turns] for q in range(2)]
    settle(0, 0, 0)
    far, plane = [], [[], []]
    for q in range(2):
        hop[q].wait_recv()
        far.append([w.post(cut(q, 1, 0, 0), cut(q, 1, 4 - k, 0), dims[q][0], k) for k in turns])
        plane[q] += [w.post(cut(q, both, 0, 0), cut(q, both, 0, 4 - k), dims[q][1], k) for k in turns]
    settle(1, 0, 0)
    for i in range(3):
        r = 4 - turns[i]
        for q in range(2):
            near[q][i].wait_recv()
            far[q][i].wait_recv()
            plane[q] += [w.post(cut(q, both, r, 0), cut(q, both, r, 4 - k), dims[q][1], k) for k in turns]
    for q in range(2):
        for copy in plane[q]:
            copy.wait_recv()

    @pl.loop(0, 30)
    def _(i):
        i = i + 1 + i // 15
        settle(i // 16, (i // 4) % 4, i % 4)

    wo_load.wait()

    def half(core):
        total = jnp.zeros((ROWS, 256), F32)
        col = pl.multiple_of(core * 256, 256)

        def step(i, total):
            lhs = jnp.concatenate(
                [LH[pl.ds(pl.multiple_of((i * 8 + j) * ROWS, ROWS), ROWS), :].astype(BF16) for j in range(8)], axis=1
            )
            rhs = wo[pl.ds(pl.multiple_of(i * 1024, 1024), 1024), pl.ds(col, 256)]
            return total + jnp.dot(lhs, rhs, preferred_element_type=F32)

        return lax.fori_loop(0, 4, step, total)

    half_out[...] = half(1 - sub).astype(BF16)
    swap = w.post(half_out, half_in, None, 0)
    mine = half(sub)
    swap.wait_recv()
    return mine + half_in[...].astype(F32)


def ffn_kernel(q_ref, nk_ref, nv_ref, kc_hbm, vc_hbm, len_ref, res_ref, wo_hbm, gain_ref, wg_hbm, wu_hbm, wd_hbm, out_ref,
               kc, vc, wo, qs, CB, LH, half_out, half_in, mid_ref,
               XB, PB, SB, RB, FB, G1, G3, HB, JB, sqs, sqr, wg, wu, wd, acc, hid, wsem, send, recv):
    at, sub = place()
    x0, y0, z0 = at
    grp = lax.rem(x0, 2)
    w = Wires(at, sub, send, recv)
    pairs = ((wg_hbm, wg), (wu_hbm, wu), (wd_hbm, wd), (kc_hbm, kc), (vc_hbm, vc), (wo_hbm, wo))
    loads = [pltpu.make_async_copy(a, b, wsem.at[i]) for i, (a, b) in enumerate(pairs)]
    loads = [loads[i] for i in (3, 4, 5, 0, 1, 2)]
    for load in loads:
        load.start()
    barrier = pltpu.get_barrier_semaphore()
    for dim in range(3):
        for by in (1, 2, 3):
            pl.semaphore_signal(barrier, inc=1, device_id=device(shifted(at, dim, by), sub), device_id_type=MESH)
    pl.semaphore_signal(barrier, inc=1, device_id=device(at, 1 - sub), device_id_type=MESH)

    loads[0].wait()
    loads[1].wait()
    attention(q_ref, nk_ref, nv_ref, kc, vc, len_ref, qs, CB)
    pl.semaphore_wait(barrier, 10)
    mid = project(w, at, sub, CB, LH, wo, loads[2], half_out, half_in) + res_ref[...].astype(F32)
    mid_ref[...] = mid
    loads = loads[3:]

    rows = (mid * gain_ref[...].astype(F32)).astype(BF16)
    XB[0, 0, 0, 0, 0] = rows[:, :128]
    XB[0, 0, 0, 0, 1] = rows[:, 128:]
    eye = lax.broadcasted_iota(jnp.int32, (ROWS, 256), 0) == lax.broadcasted_iota(jnp.int32, (ROWS, 256), 1)
    column = jnp.sum(mid * mid, axis=1, keepdims=True)
    sqs[0] = jnp.broadcast_to(jnp.sum(jnp.where(eye, column, 0.0), axis=0, keepdims=True), (8, 256))

    sq_copies = {}

    def sq(step):
        if step > 0:
            total = sqs[step - 1]
            for i, copy in enumerate(sq_copies[step - 1]):
                copy.wait_recv()
                total = total + sqr[(step - 1) * 3 + i]
            sqs[step] = total
        if step == 0:
            sq_copies[0] = [w.post(sqs.at[0], sqr.at[0], None, 0)]
        elif step == 1:
            sq_copies[1] = [w.post(sqs.at[1], sqr.at[3 + i], 1, k) for i, k in enumerate((1, 3, 2))]
        elif step == 2:
            sq_copies[2] = [w.post(sqs.at[2], sqr.at[6 + i], 2, k) for i, k in enumerate((1, 3, 2))]
        elif step == 3:
            sq_copies[3] = [w.post(sqs.at[3], sqr.at[9], 0, 2)]
        else:
            sq_copies[4] = [w.post(sqs.at[4], sqr.at[12], 0, 1)]

    def dev_at(rx, ry, rz):
        return (lax.rem(x0 + rx, 4) // 2) * 16 + lax.rem(z0 + rz, 4) * 4 + lax.rem(y0 + ry, 4)

    def ready(step):
        if step != 2:
            return
        loads[0].wait()
        loads[1].wait()
        acc[...] = jnp.zeros_like(acc)

        @pl.loop(0, 8)
        def _(i):
            rx, ry = (i // 4) * 2, i % 4
            other = lax.rem(rx + 5 - 2 * grp, 4)
            ks = [pl.multiple_of(dev_at(rx, ry, rz) * 512, 512) for rz in range(4)]
            lhs = jnp.concatenate(
                [
                    jnp.concatenate([XB[q, ry, rz, s, h] for rz in range(4) for s in (sub, 1 - sub) for h in (0, 1)], axis=1)
                    for q in (rx, other)
                ],
                axis=0,
            )
            for j, weight in enumerate((wg, wu)):
                rhs = jnp.concatenate([weight[:, pl.ds(k, 512)] for k in ks], axis=1)
                acc[j] += lax.dot_general(lhs, rhs, (((1,), (1,)), ((), ())), preferred_element_type=F32)

    gather(w, XB, sq, ready)

    sq_copies[4][0].wait_recv()
    for i, sums in enumerate((sqs[4], sqr[12])):
        inv_row = lax.rsqrt(sums[0:1] / D + 1e-05)
        inv = jnp.sum(jnp.where(eye, inv_row, 0.0), axis=1, keepdims=True)
        gate = acc[0, i * ROWS:(i + 1) * ROWS] * inv
        up = acc[1, i * ROWS:(i + 1) * ROWS] * inv
        hid[i] = (gate / (1.0 + jnp.exp(-gate)) * up).astype(BF16)
    loads[2].wait()
    scatter(w, dev_at, sub, hid, wd, PB, SB, RB, FB, G1, G3, HB, JB)
    out_ref[...] = (mid_ref[...] + jnp.concatenate([PB[0, 0, 0, 0], PB[0, 0, 0, 1]], axis=1).astype(F32)).astype(BF16)
    w.drain()


def scatter(w, dev_at, sub, hid, wd, PB, SB, RB, FB, G1, G3, HB, JB):
    def blocks(count, where, target, core, extra):
        @pl.loop(0, count, unroll=4 if count % 4 == 0 else 3)
        def _(i):
            rx, ry, rz = where(i)
            col = pl.multiple_of(dev_at(rx, ry, rz) * 512 + core * 256, 256)
            part = jnp.dot(hid[lax.rem(rx, 2)], wd[:, pl.ds(col, 256)], preferred_element_type=F32)
            for h in (0, 1):
                one = part[:, h * 128:(h + 1) * 128]
                if extra is not None:
                    one = one + extra[rx, ry, rz, h].astype(F32)
                target[rx, ry, rz, h] = one.astype(BF16)

    def add(target, sources, p, count, where, half=None):
        _, h, (r0, r1), halves = PARTS[p]
        if half is not None:
            h, (r0, r1) = halves[half]
        hs = (0, 1) if isinstance(h, slice) else (h,)

        def one(i):
            t, ss = where(i)
            for hh in hs:
                total = target[tuple(t) + (hh, slice(r0, r1))].astype(F32)
                for source, s in zip(sources, ss):
                    total = total + source[tuple(s) + (hh, slice(r0, r1))].astype(F32)
                target[tuple(t) + (hh, slice(r0, r1))] = total.astype(BF16)

        if count == 1:
            one(0)
        else:
            pl.loop(0, count, unroll=count)(one)

    def cell(c, i):
        return {"0": (0, 0), "1": (i + 1, 0), "2": (0, i + 1), "3": (i + 1, 1), "4": (i + 1, 2), "5": (i + 1, 3)}[c]

    count = {"0": 1, "1": 3, "2": 3, "3": 3, "4": 3, "5": 3}

    def spot(p, a, b, c):
        dims = PARTS[p][0]
        r = [None] * 3
        r[dims[0]], r[dims[1]], r[dims[2]] = a, b, c
        return tuple(r)

    skip = lambda v: v + v // 2
    near = (slice(0, 2), 3)
    sets = (
        (16, lambda i: (2, i // 4, i % 4), [(2, slice(0, 4), slice(0, 4))]),
        (12, lambda i: (skip(i // 4), i % 4, 2), [(a, slice(0, 4), 2) for a in near]),
        (9, lambda i: (skip(i // 3), 2, skip(i % 3)), [(a, 2, c) for a in near for c in near]),
        (27, lambda i: (skip(i // 9), skip((i // 3) % 3), skip(i % 3)), [(a, b, c) for a in near for b in near for c in near]),
    )
    swap = {}

    def far_core(n):
        total, where, slices = sets[n]
        blocks(total, where, SB, 1 - sub, None)
        swap[n] = [w.post(SB.at[idx], RB.at[idx], None, 0) for idx in slices]

    def near_core(n):
        for copy in swap[n]:
            copy.wait_recv()
        total, where, _ = sets[n]
        blocks(total, where, PB, sub, RB)

    first, second, third, fourth = {}, {}, {}, {}
    order = "435210"

    def start(p):
        d3 = PARTS[p][0][2]
        for c in order:
            a, b = CHUNKS[c]
            first[p, c] = [
                w.post(block(PB, p, a, b, 2, half=0), flat(FB, p, lay(p, a, b), 0), d3, 1),
                w.post(block(PB, p, a, b, 2, half=1), flat(FB, p, lay(p, a, b), 1), d3, 3),
            ]

    far_core(0)
    far_core(1)
    near_core(0)
    start(1)
    far_core(2)
    near_core(1)
    start(0)
    near_core(2)
    start(2)
    far_core(3)
    near_core(3)

    def pass_on(c):
        a, b = CHUNKS[c]
        for p in (1, 0, 2):
            d3 = PARTS[p][0][2]
            for q, c3 in ((0, 1), (1, 3)):
                first[p, c][q].wait_recv()
                add(PB, (FB,), p, count[c], lambda i: (spot(p, *cell(c, i), c3), (lay(p, *cell(c, i)),)), half=q)
            second[p, c] = [
                w.post(block(PB, p, a, b, 1), flat(G1, p, lay(p, a, b)), d3, 1),
                w.post(block(PB, p, a, b, 3), flat(G3, p, lay(p, a, b)), d3, 3),
            ]

    def collect(c):
        a, b = CHUNKS[c]
        for p in (1, 0, 2):
            d2 = PARTS[p][0][1]
            for copy in second[p, c]:
                copy.wait_recv()
            add(PB, (G1, G3), p, count[c], lambda i: (spot(p, *cell(c, i), 0), (lay(p, *cell(c, i)),) * 2))
            if c in "345":
                third[p, b] = w.post(block(PB, p, a, b, 0), flat(HB, p, (b - 1, a)), d2, b)
            if c == "2":
                third[p, 0] = [w.post(block(PB, p, 0, k, 0), flat(HB, p, (k - 1, 0)), d2, k) for k in (1, 3, 2)]

    for c in order:
        pass_on(c)
    for c in order:
        collect(c)
    for p in (1, 0, 2):
        d1 = PARTS[p][0][0]
        for k in (2, 1, 3):
            third[p, k].wait_recv()
        add(PB, (HB,) * 3, p, 3, lambda i: (spot(p, i + 1, 0, 0), tuple((k, i + 1) for k in range(3))))
        fourth[p] = [w.post(block(PB, p, k, 0, 0), flat(JB, p, (k - 1,)), d1, k) for k in (1, 3, 2)]
    for p in (1, 0, 2):
        for copy in third[p, 0]:
            copy.wait_recv()
        add(PB, (HB,) * 3, p, 1, lambda i: (spot(p, 0, 0, 0), tuple((k, 0) for k in range(3))))
    for p in (1, 0, 2):
        for copy in fourth[p]:
            copy.wait_recv()
        add(PB, (JB,) * 3, p, 1, lambda i: (spot(p, 0, 0, 0), tuple((k,) for k in range(3))))


def ffn(q, nk, nv, kc, vc, lengths, res, wo, gain, wg, wu, wd):
    hbm = pl.BlockSpec(memory_space=pl.ANY)
    vmem = pl.BlockSpec(memory_space=pltpu.VMEM)
    smem = pl.BlockSpec(memory_space=pltpu.SMEM)
    grid = (4, 4, 4)
    tail = (2, ROWS, 128)
    return pl.pallas_call(
        ffn_kernel,
        out_shape=jax.ShapeDtypeStruct((ROWS, 256), BF16),
        in_specs=[vmem, vmem, vmem, hbm, hbm, smem, vmem, hbm, vmem, hbm, hbm, hbm],
        out_specs=vmem,
        scratch_shapes=[
            pltpu.VMEM((5, CACHE, 256), BF16),
            pltpu.VMEM((5, CACHE, 256), BF16),
            pltpu.VMEM((4096, 512), BF16),
            pltpu.VMEM((ROWS, 128), F32),
            pltpu.VMEM((2, 4, 4, ROWS, 128), BF16),
            pltpu.VMEM((32 * ROWS, 128), F32),
            pltpu.VMEM((ROWS, 256), BF16),
            pltpu.VMEM((ROWS, 256), BF16),
            pltpu.VMEM((ROWS, 256), F32),
            pltpu.VMEM(grid + (2,) + tail, BF16),
            pltpu.VMEM(grid + tail, BF16),
            pltpu.VMEM(grid + tail, BF16),
            pltpu.VMEM(grid + tail, BF16),
            pltpu.VMEM((4, 4) + tail, BF16),
            pltpu.VMEM((4, 4) + tail, BF16),
            pltpu.VMEM((4, 4) + tail, BF16),
            pltpu.VMEM((3, 4) + tail, BF16),
            pltpu.VMEM((3,) + tail, BF16),
            pltpu.VMEM((5, 8, 256), F32),
            pltpu.VMEM((13, 8, 256), F32),
            pltpu.VMEM((HID, D), BF16),
            pltpu.VMEM((HID, D), BF16),
            pltpu.VMEM((HID, D), BF16),
            pltpu.VMEM((2, 2 * ROWS, HID), F32),
            pltpu.VMEM((2, ROWS, HID), BF16),
            pltpu.SemaphoreType.DMA((6,)),
            pltpu.SemaphoreType.DMA((300,)),
            pltpu.SemaphoreType.DMA((300,)),
        ],
        compiler_params=pltpu.CompilerParams(
            collective_id=1, has_side_effects=True, vmem_limit_bytes=62 * 2**20
        ),
        name="ffn",
    )(q, nk, nv, kc, vc, lengths, res, wo, gain, wg, wu, wd)


def shards(
    queries,
    new_keys,
    new_values,
    key_cache,
    value_cache,
    lengths,
    residual,
    o_weight,
    norm_gain,
    w_gate,
    w_up,
    w_down,
):
    return ffn(
        queries, new_keys, new_values, key_cache, value_cache, lengths, residual,
        o_weight, norm_gain[None, :], w_gate, w_up, w_down,
    )


def solution(mesh):
    placed = (
        P(("grp", "dev"), "sub"),
        P(("grp", "dev"), "sub"),
        P(("grp", "dev"), "sub"),
        P(("grp", "dev"), None, "sub"),
        P(("grp", "dev"), None, "sub"),
        P(("grp", "dev")),
        P("grp", ("dev", "sub")),
        P("sub", "dev"),
        P(("dev", "sub")),
        P(("grp", "dev", "sub"), None),
        P(("grp", "dev", "sub"), None),
        P(("grp", "dev", "sub"), None),
    )
    return jax.shard_map(
        shards, mesh=mesh, in_specs=placed, out_specs=P("grp", ("dev", "sub")), check_vma=False
    )
```

time: 247 us -> 113 us (0.46); the launches traced: 245 us -> 113 us
  waiting for transfers between devices: 81.2 us -> 0 us
  Pallas kernels: 134 us -> 110 us
  between operations: 13.5 us -> 0.01 us
  matrix products: 5.9 us -> 0 us
  local copies, waits for them, and re-layouts: 6.9 us -> 2.75 us
  other arithmetic: 2.61 us -> 0 us
    all_gather x1 -> x0, waiting for transfers between devices: 73.3 us -> none  [shards(): lax.all_gather(context, 'dev', axis=0, tiled=True)]
    pallas_call x1, Pallas kernels: 134 us -> 110 us  [ffn(): pl.pallas_call(ffn_kernel, out_shape=jax.ShapeDtypeStruct((ROWS, 256), BF...]
    reduce_scatter x1 -> x0, waiting for transfers between devices: 7.86 us -> none  [shards(): lax.psum_scatter(partial_out.astype(jnp.bfloat16), 'sub', scatter_dimensi...]
    dot_general x4 -> x0, matrix products: 5.9 us -> none  [the longest x1 3.7 us: shards(): jnp.dot(lax.all_gather(context, 'dev', axis=0, tiled=True), o_weight, pre...]
    unnamed x10 -> x1, local copies, waits for them, and re-layouts: 4.93 us -> 1.53 us
  transfers between devices with their start and end apart: 2 -> 0, of which waited for: 2 -> 0; matrix products, arithmetic and copies ran while one was open for 0% -> 0% of each run, Pallas kernels for 0% -> 0%
where the time goes in v2:
time: 113 us
  Pallas kernels  110 us (97%)
  local copies, waits for them, and re-layouts  2.75 us (2%)
    pallas_call x1, Pallas kernels, ffn(): pl.pallas_call(ffn_kernel, out_shape=jax.ShapeDtypeStruct((ROWS, 256), BF...  110 us

profile of v2, /device:TPU:0, one launch (start us, length us, event | category | flops | bytes accessed | tf_op | source)
XLA Modules:
  0.0 113.1 jit_solution(15258354367153275749)
XLA Ops:
  0.0 1.2 %broadcast_in_dim.3.gain_ref = bf16[1,256]{1,0:T(2,128)(2,1)} reshape(bf16[256]{0:T(256)(128)(2,1)} %param.20) | data formatting | bytes 1024 | tf_op jit(solution)/shard_map/broadcast_in_dim | solution.py:549
  1.2 110.3 %ffn.1 = bf16[160,256]{1,0:T(8,128)(2,1)} custom-call(bf16[5,4096]{1,0:T(8,128)(2,1)} %q_ref.1, bf16[5,256]{1,0:T(8,128)(2,1)} %nk_ref.1, bf16[5,256]{1,0:T(8,128)(2,1)} %nv_ref.1, bf16[5,384,256]{2,1,0:T(8,128)(2,1)} %kc_hbm.1, bf16[5,384,256]{2,1,0:T(8,128)(2,1)} %vc_hbm.1, s32[5]{0:T(128)} %len_ref.1, bf16[160,256]{1,0:T(8,128)(2,1)} %res_ref.1, ...), custom_call_target="tpu_custom_call" | custom-call | tf_op jit(solution)/shard_map/ffn/pallas_call | solution.py:491
  111.5 1.5 %copy.14 = bf16[160,256]{1,0:T(8,128)(2,1)} copy(bf16[160,256]{1,0:T(8,128)(2,1)} %ffn.1) | data formatting | bytes 163840

commit v3 on v2

--- a/solution.py
+++ b/solution.py
@@ -16,6 +16,7 @@
     "0": (0, 0), "1": (slice(1, 4), 0), "2": (0, slice(1, 4)),
     "3": (slice(1, 4), 1), "4": (slice(1, 4), 2), "5": (slice(1, 4), 3),
 }
+FLIP = {"0": 0, "1": 1, "2": 0, "3": 0, "4": 1, "5": 0}
 PARTS = (
     ((0, 1, 2), 0, (0, 112), ((0, (0, 64)), (0, (64, 112)))),
     ((1, 2, 0), 1, (0, 112), ((1, (0, 64)), (1, (64, 112)))),
@@ -58,6 +59,10 @@
         self.started.append(copy)
         return copy
 
+    def sent(self, copy):
+        copy.wait_send()
+        self.started = [c for c in self.started if c is not copy]
+
     def drain(self):
         for copy in self.started:
             copy.wait_send()
@@ -101,12 +106,17 @@
     def onward(p, c):
         a, b = CHUNKS[c]
         d3 = PARTS[p][0][2]
+        f = FLIP[c]
         for copy in m3[p, c]:
             copy.wait_recv()
         fwd[p, c] = [
-            w.post(xb(p, a, b, 3, 0), xb(p, a, b, 2, 0), d3, 1),
-            w.post(xb(p, a, b, 1, 1), xb(p, a, b, 2, 1), d3, 3),
+            w.post(xb(p, a, b, 3, f), xb(p, a, b, 2, f), d3, 1),
+            w.post(xb(p, a, b, 1, 1 - f), xb(p, a, b, 2, 1 - f), d3, 3),
         ]
+
+    def landed(copies):
+        for copy in copies:
+            copy.wait_recv()
 
     def across(p, a, b, c):
         d2d.append(w.post(xb(p, a, b, c), xb(p, a, b, c, s=1), None, 0))
@@ -125,45 +135,59 @@
         for copy in m1[p]:
             copy.wait_recv()
         m2b[p] = [w.post(xb(p, slice(1, 4), 0, 0), xb(p, slice(1, 4), 4 - k, 0), d2, k) for k in (1, 3, 2)]
+    for p in range(3):
         plane(p, "1")
-        across(p, slice(0, 4), 0, 0)
     for p in range(3):
         for copy in m2a[p]:
             copy.wait_recv()
         plane(p, "2")
+        across(p, slice(0, 4), 0, 0)
     sq(1)
     for p in range(3):
         onward(p, "0")
-    for i, c in enumerate("534"):
+    for i, c in enumerate("53"):
         for p in range(3):
             m2b[p][i].wait_recv()
             plane(p, c)
-        if i == 0:
-            for p in range(3):
-                onward(p, "1")
     sq(2)
     for p in range(3):
+        m2b[p][2].wait_recv()
+        plane(p, "4")
         across(p, slice(0, 4), slice(1, 4), 0)
-        onward(p, "2")
-    ready(0)
-    sq(3)
-    for c in "534":
+    for c in "12":
         for p in range(3):
             onward(p, c)
-    for p in range(3):
-        across(p, slice(0, 4), slice(0, 4), 1)
-        across(p, slice(0, 4), slice(0, 4), 3)
+    sq(3)
+    for p in range(3):
+        onward(p, "5")
+    for p in range(3):
+        for c in "012":
+            for copy in fwd[p, c]:
+                copy.wait_recv()
+        across(p, slice(0, 4), 0, slice(1, 4))
+        across(p, 0, slice(1, 4), slice(1, 4))
+    early = list(d2d)
+    d2d.clear()
+    for p in range(3):
+        onward(p, "3")
+    for p in range(3):
+        onward(p, "4")
+        across(p, slice(1, 4), slice(1, 4), 1)
+        across(p, slice(1, 4), slice(1, 4), 3)
     sq(4)
-    ready(1)
-    for chunks, r2 in (("01", 0), ("25", 3), ("3", 1), ("4", 2)):
+    landed(early)
+    for step in range(4):
+        ready(step)
+    landed(d2d)
+    ready(4)
+    for r2, c in ((3, "5"), (1, "3"), (2, "4")):
         for p in range(3):
-            for c in chunks:
-                for copy in fwd[p, c]:
-                    copy.wait_recv()
-            across(p, slice(0, 4), r2, 2)
-    for copy in d2d:
-        copy.wait_recv()
-    ready(2)
+            for copy in fwd[p, c]:
+                copy.wait_recv()
+            across(p, slice(1, 4), r2, 2)
+    landed(d2d[6:])
+    for step in (5, 6, 7, 8):
+        ready(step)
 
 
 def attention(q_ref, nk_ref, nv_ref, kc, vc, len_ref, qs, CB):
@@ -192,7 +216,7 @@
             CB[0, 0, 0, b * 32 + g * 16:b * 32 + (g + 1) * 16] = context.astype(BF16)
 
 
-def project(w, at, sub, CB, LH, wo, wo_load, half_out, half_in):
+def project(w, at, sub, CB, LH, wo, wo_load, half_out, half_in, mid_ref):
     x0, y0, z0 = at
 
     def part(q, rx, ry, rz):
@@ -210,23 +234,33 @@
         for b in range(5):
             LH[pl.ds(dev * 5 + b, 32, stride=ROWS), :] = CB[rx, ry, rz, b * 32:(b + 1) * 32].astype(F32)
 
+    planes = [[], []]
+
+    def plane(q, rx, r):
+        planes[q] += [w.post(cut(q, rx, r, 0), cut(q, rx, r, 4 - k), dims[q][1], k) for k in turns]
+
     hop = [w.post(part(q, 0, 0, 0), part(q, 1, 0, 0), 0, 2) for q in range(2)]
     near = [[w.post(cut(q, 0, 0, 0), cut(q, 0, 4 - k, 0), dims[q][0], k) for k in turns] for q in range(2)]
+    for q in range(2):
+        plane(q, 0, 0)
     settle(0, 0, 0)
-    far, plane = [], [[], []]
+    far = []
     for q in range(2):
         hop[q].wait_recv()
         far.append([w.post(cut(q, 1, 0, 0), cut(q, 1, 4 - k, 0), dims[q][0], k) for k in turns])
-        plane[q] += [w.post(cut(q, both, 0, 0), cut(q, both, 0, 4 - k), dims[q][1], k) for k in turns]
+    for i in range(3):
+        for q in range(2):
+            near[q][i].wait_recv()
+            plane(q, 0, 4 - turns[i])
+    for q in range(2):
+        plane(q, 1, 0)
     settle(1, 0, 0)
     for i in range(3):
-        r = 4 - turns[i]
         for q in range(2):
-            near[q][i].wait_recv()
             far[q][i].wait_recv()
-            plane[q] += [w.post(cut(q, both, r, 0), cut(q, both, r, 4 - k), dims[q][1], k) for k in turns]
+            plane(q, 1, 4 - turns[i])
     for q in range(2):
-        for copy in plane[q]:
+        for copy in planes[q]:
             copy.wait_recv()
 
     @pl.loop(0, 30)
@@ -236,22 +270,19 @@
 
     wo_load.wait()
 
-    def half(core):
-        total = jnp.zeros((ROWS, 256), F32)
-        col = pl.multiple_of(core * 256, 256)
-
-        def step(i, total):
-            lhs = jnp.concatenate(
-                [LH[pl.ds(pl.multiple_of((i * 8 + j) * ROWS, ROWS), ROWS), :].astype(BF16) for j in range(8)], axis=1
-            )
-            rhs = wo[pl.ds(pl.multiple_of(i * 1024, 1024), 1024), pl.ds(col, 256)]
-            return total + jnp.dot(lhs, rhs, preferred_element_type=F32)
-
-        return lax.fori_loop(0, 4, step, total)
-
-    half_out[...] = half(1 - sub).astype(BF16)
-    swap = w.post(half_out, half_in, None, 0)
-    mine = half(sub)
+    def step(i, total):
+        lhs = jnp.concatenate(
+            [LH[pl.ds(pl.multiple_of((i * 8 + j) * ROWS, ROWS), ROWS), :].astype(BF16) for j in range(8)], axis=1
+        )
+        rhs = wo[pl.ds(pl.multiple_of(i * 1024, 1024), 1024), :]
+        return total + jnp.dot(lhs, rhs, preferred_element_type=F32)
+
+    total = lax.fori_loop(0, 4, step, jnp.zeros((ROWS, 512), F32))
+    for core in range(2):
+        half_out[core] = total[:, core * 256:(core + 1) * 256].astype(BF16)
+        mid_ref[core] = total[:, core * 256:(core + 1) * 256]
+    swap = w.post(half_out.at[1 - sub], half_in, None, 0)
+    mine = mid_ref[sub]
     swap.wait_recv()
     return mine + half_in[...].astype(F32)
 
@@ -278,11 +309,11 @@
     loads[1].wait()
     attention(q_ref, nk_ref, nv_ref, kc, vc, len_ref, qs, CB)
     pl.semaphore_wait(barrier, 10)
-    mid = project(w, at, sub, CB, LH, wo, loads[2], half_out, half_in) + res_ref[...].astype(F32)
-    mid_ref[...] = mid
+    mid = project(w, at, sub, CB, LH, wo, loads[2], half_out, half_in, mid_ref) + res_ref[...].astype(F32)
+    mid_ref[0] = mid
     loads = loads[3:]
 
-    rows = (mid * gain_ref[...].astype(F32)).astype(BF16)
+    rows = (mid * gain_ref[...].astype(F32)[None, :]).astype(BF16)
     XB[0, 0, 0, 0, 0] = rows[:, :128]
     XB[0, 0, 0, 0, 1] = rows[:, 128:]
     eye = lax.broadcasted_iota(jnp.int32, (ROWS, 256), 0) == lax.broadcasted_iota(jnp.int32, (ROWS, 256), 1)
@@ -312,28 +343,31 @@
     def dev_at(rx, ry, rz):
         return (lax.rem(x0 + rx, 4) // 2) * 16 + lax.rem(z0 + rz, 4) * 4 + lax.rem(y0 + ry, 4)
 
+    corner = [(r, 0, rz) for r in (0, 2) for rz in range(4)] + [(r, ry, 0) for r in (0, 2) for ry in (1, 2, 3)]
+    odd = [(0, ry, rz) for ry in (1, 3) for rz in (1, 3)]
+    last = [(r, ry, rz) for r in (0, 2) for ry in (1, 2, 3) for rz in (1, 2, 3) if r or ry == 2 or rz == 2]
+    batches = {0: corner[0:4], 1: corner[4:8], 2: corner[8:11], 3: corner[11:14], 4: odd,
+               5: last[0:4], 6: last[4:8], 7: last[8:11], 8: last[11:14]}
+
     def ready(step):
-        if step != 2:
-            return
-        loads[0].wait()
-        loads[1].wait()
-        acc[...] = jnp.zeros_like(acc)
-
-        @pl.loop(0, 8)
-        def _(i):
-            rx, ry = (i // 4) * 2, i % 4
-            other = lax.rem(rx + 5 - 2 * grp, 4)
-            ks = [pl.multiple_of(dev_at(rx, ry, rz) * 512, 512) for rz in range(4)]
-            lhs = jnp.concatenate(
-                [
-                    jnp.concatenate([XB[q, ry, rz, s, h] for rz in range(4) for s in (sub, 1 - sub) for h in (0, 1)], axis=1)
-                    for q in (rx, other)
-                ],
-                axis=0,
-            )
-            for j, weight in enumerate((wg, wu)):
-                rhs = jnp.concatenate([weight[:, pl.ds(k, 512)] for k in ks], axis=1)
-                acc[j] += lax.dot_general(lhs, rhs, (((1,), (1,)), ((), ())), preferred_element_type=F32)
+        if step == 0:
+            loads[0].wait()
+            loads[1].wait()
+        pairs = [(rx, lax.rem(rx + 5 - 2 * grp, 4), ry, rz) for rx, ry, rz in batches[step]]
+        ks = [pl.multiple_of(dev_at(rx, ry, rz) * 512, 512) for rx, _, ry, rz in pairs]
+        lhs = jnp.concatenate(
+            [
+                jnp.concatenate(
+                    [XB[pair[q], pair[2], pair[3], s, h] for pair in pairs for s in (sub, 1 - sub) for h in (0, 1)], axis=1
+                )
+                for q in (0, 1)
+            ],
+            axis=0,
+        )
+        for j, weight in enumerate((wg, wu)):
+            rhs = jnp.concatenate([weight[:, pl.ds(k, 512)] for k in ks], axis=1)
+            part = lax.dot_general(lhs, rhs, (((1,), (1,)), ((), ())), preferred_element_type=F32)
+            acc[j] = part if step == 0 else acc[j] + part
 
     gather(w, XB, sq, ready)
 
@@ -346,22 +380,21 @@
         hid[i] = (gate / (1.0 + jnp.exp(-gate)) * up).astype(BF16)
     loads[2].wait()
     scatter(w, dev_at, sub, hid, wd, PB, SB, RB, FB, G1, G3, HB, JB)
-    out_ref[...] = (mid_ref[...] + jnp.concatenate([PB[0, 0, 0, 0], PB[0, 0, 0, 1]], axis=1).astype(F32)).astype(BF16)
+    out_ref[...] = (mid_ref[0] + jnp.concatenate([PB[0, 0, 0, 0], PB[0, 0, 0, 1]], axis=1).astype(F32)).astype(BF16)
     w.drain()
 
 
 def scatter(w, dev_at, sub, hid, wd, PB, SB, RB, FB, G1, G3, HB, JB):
-    def blocks(count, where, target, core, extra):
-        @pl.loop(0, count, unroll=4 if count % 4 == 0 else 3)
-        def _(i):
-            rx, ry, rz = where(i)
+    def blocks(rx, ry, target, core, extra):
+        @pl.loop(0, 4, unroll=4)
+        def _(rz):
             col = pl.multiple_of(dev_at(rx, ry, rz) * 512 + core * 256, 256)
-            part = jnp.dot(hid[lax.rem(rx, 2)], wd[:, pl.ds(col, 256)], preferred_element_type=F32)
+            part = jnp.dot(hid[rx % 2], wd[:, pl.ds(col, 256)], preferred_element_type=F32)
             for h in (0, 1):
                 one = part[:, h * 128:(h + 1) * 128]
                 if extra is not None:
-                    one = one + extra[rx, ry, rz, h].astype(F32)
-                target[rx, ry, rz, h] = one.astype(BF16)
+                    one = one + extra[rz, h].astype(F32)
+                target[rz, h] = one.astype(BF16)
 
     def add(target, sources, p, count, where, half=None):
         _, h, (r0, r1), halves = PARTS[p]
@@ -393,61 +426,67 @@
         r[dims[0]], r[dims[1]], r[dims[2]] = a, b, c
         return tuple(r)
 
-    skip = lambda v: v + v // 2
-    near = (slice(0, 2), 3)
-    sets = (
-        (16, lambda i: (2, i // 4, i % 4), [(2, slice(0, 4), slice(0, 4))]),
-        (12, lambda i: (skip(i // 4), i % 4, 2), [(a, slice(0, 4), 2) for a in near]),
-        (9, lambda i: (skip(i // 3), 2, skip(i % 3)), [(a, 2, c) for a in near for c in near]),
-        (27, lambda i: (skip(i // 9), skip((i // 3) % 3), skip(i % 3)), [(a, b, c) for a in near for b in near for c in near]),
-    )
-    swap = {}
-
-    def far_core(n):
-        total, where, slices = sets[n]
-        blocks(total, where, SB, 1 - sub, None)
-        swap[n] = [w.post(SB.at[idx], RB.at[idx], None, 0) for idx in slices]
-
-    def near_core(n):
-        for copy in swap[n]:
-            copy.wait_recv()
-        total, where, _ = sets[n]
-        blocks(total, where, PB, sub, RB)
-
     first, second, third, fourth = {}, {}, {}, {}
-    order = "435210"
-
-    def start(p):
-        d3 = PARTS[p][0][2]
-        for c in order:
+    order = "435120"
+    units = [(2, 2), (2, 1), (2, 3), (2, 0), (3, 2), (1, 2), (0, 2), (3, 3), (1, 3), (3, 1), (1, 1), (0, 1), (0, 3), (3, 0), (1, 0), (0, 0)]
+    swap, waiting = {}, []
+    for c in order:
+        for p in (1, 2, 0):
+            for c3 in (2, 1, 3):
+                need = set()
+                for i in range(count[c]):
+                    need.add(spot(p, *cell(c, i), c3)[:2])
+                waiting.append((c3 != 2, p, c, c3, need))
+    waiting.sort(key=lambda m: m[0])
+
+    def far_core(u):
+        rx, ry = units[u]
+        if u >= 8:
+            w.sent(swap[u - 8])
+        blocks(rx, ry, SB.at[u % 8], 1 - sub, None)
+        swap[u] = w.post(SB.at[u % 8], RB.at[rx, ry], None, 0)
+
+    def near_core(u):
+        swap[u].wait_recv()
+        rx, ry = units[u]
+        blocks(rx, ry, PB.at[rx, ry], sub, RB.at[rx, ry])
+        done = set(units[:u + 1])
+        for message in list(waiting):
+            _, p, c, c3, need = message
+            if not need <= done:
+                continue
+            waiting.remove(message)
             a, b = CHUNKS[c]
-            first[p, c] = [
-                w.post(block(PB, p, a, b, 2, half=0), flat(FB, p, lay(p, a, b), 0), d3, 1),
-                w.post(block(PB, p, a, b, 2, half=1), flat(FB, p, lay(p, a, b), 1), d3, 3),
-            ]
-
-    far_core(0)
-    far_core(1)
-    near_core(0)
-    start(1)
-    far_core(2)
-    near_core(1)
-    start(0)
-    near_core(2)
-    start(2)
-    far_core(3)
-    near_core(3)
+            d3 = PARTS[p][0][2]
+            lead, f = lay(p, a, b), FLIP[c]
+            if c3 == 2:
+                first[p, c] = [
+                    w.post(block(PB, p, a, b, 2, half=f), flat(FB, p, lead, f), d3, 1),
+                    w.post(block(PB, p, a, b, 2, half=1 - f), flat(FB, p, lead, 1 - f), d3, 3),
+                ]
+            elif c3 == 1:
+                second.setdefault((p, c), []).append(w.post(block(PB, p, a, b, 1, half=1 - f), flat(G1, p, lead, 1 - f), d3, 1))
+            else:
+                second.setdefault((p, c), []).append(w.post(block(PB, p, a, b, 3, half=f), flat(G3, p, lead, f), d3, 3))
+
+    lag = 4
+    for u in range(16 + lag):
+        if u < 16:
+            far_core(u)
+        if u >= lag:
+            near_core(u - lag)
 
     def pass_on(c):
         a, b = CHUNKS[c]
         for p in (1, 0, 2):
             d3 = PARTS[p][0][2]
+            f = FLIP[c]
             for q, c3 in ((0, 1), (1, 3)):
                 first[p, c][q].wait_recv()
-                add(PB, (FB,), p, count[c], lambda i: (spot(p, *cell(c, i), c3), (lay(p, *cell(c, i)),)), half=q)
-            second[p, c] = [
-                w.post(block(PB, p, a, b, 1), flat(G1, p, lay(p, a, b)), d3, 1),
-                w.post(block(PB, p, a, b, 3), flat(G3, p, lay(p, a, b)), d3, 3),
+                add(PB, (FB,), p, count[c], lambda i: (spot(p, *cell(c, i), c3), (lay(p, *cell(c, i)),)), half=q ^ f)
+            second[p, c] += [
+                w.post(block(PB, p, a, b, 1, half=f), flat(G1, p, lay(p, a, b), f), d3, 1),
+                w.post(block(PB, p, a, b, 3, half=1 - f), flat(G3, p, lay(p, a, b), 1 - f), d3, 3),
             ]
 
     def collect(c):
@@ -500,12 +539,12 @@
             pltpu.VMEM((ROWS, 128), F32),
             pltpu.VMEM((2, 4, 4, ROWS, 128), BF16),
             pltpu.VMEM((32 * ROWS, 128), F32),
+            pltpu.VMEM((2, ROWS, 256), BF16),
             pltpu.VMEM((ROWS, 256), BF16),
-            pltpu.VMEM((ROWS, 256), BF16),
-            pltpu.VMEM((ROWS, 256), F32),
+            pltpu.VMEM((2, ROWS, 256), F32),
             pltpu.VMEM(grid + (2,) + tail, BF16),
             pltpu.VMEM(grid + tail, BF16),
-            pltpu.VMEM(grid + tail, BF16),
+            pltpu.VMEM((8, 4) + tail, BF16),
             pltpu.VMEM(grid + tail, BF16),
             pltpu.VMEM((4, 4) + tail, BF16),
             pltpu.VMEM((4, 4) + tail, BF16),
@@ -520,8 +559,8 @@
             pltpu.VMEM((2, 2 * ROWS, HID), F32),
             pltpu.VMEM((2, ROWS, HID), BF16),
             pltpu.SemaphoreType.DMA((6,)),
-            pltpu.SemaphoreType.DMA((300,)),
-            pltpu.SemaphoreType.DMA((300,)),
+            pltpu.SemaphoreType.DMA((360,)),
+            pltpu.SemaphoreType.DMA((360,)),
         ],
         compiler_params=pltpu.CompilerParams(
             collective_id=1, has_side_effects=True, vmem_limit_bytes=62 * 2**20
@@ -546,7 +585,7 @@
 ):
     return ffn(
         queries, new_keys, new_values, key_cache, value_cache, lengths, residual,
-        o_weight, norm_gain[None, :], w_gate, w_up, w_down,
+        o_weight, norm_gain, w_gate, w_up, w_down,
     )
 
 

time: 113 us -> 102 us (0.903)
  Pallas kernels: 110 us -> 100 us
  local copies, waits for them, and re-layouts: 2.75 us -> 1.53 us
    pallas_call x1, Pallas kernels: 110 us -> 100 us  [ffn(): pl.pallas_call(ffn_kernel, out_shape=jax.ShapeDtypeStruct((ROWS, 256), BF...]
    broadcast_in_dim x1 -> x0, local copies, waits for them, and re-layouts: 1.22 us -> none  [shards(): norm_gain[None, :]]
where the time goes in v3:
time: 102 us
  Pallas kernels  100 us (98%)
  local copies, waits for them, and re-layouts  1.53 us (2%)
    pallas_call x1, Pallas kernels, ffn(): pl.pallas_call(ffn_kernel, out_shape=jax.ShapeDtypeStruct((ROWS, 256), BF...  100 us

profile of v3, /device:TPU:0, one launch (start us, length us, event | category | flops | bytes accessed | tf_op | source)
XLA Modules:
  0.0 101.8 jit_solution(6814521709056988255)
XLA Ops:
  0.0 100.2 %ffn.1 = bf16[160,256]{1,0:T(8,128)(2,1)} custom-call(bf16[5,4096]{1,0:T(8,128)(2,1)} %q_ref.1, bf16[5,256]{1,0:T(8,128)(2,1)} %nk_ref.1, bf16[5,256]{1,0:T(8,128)(2,1)} %nv_ref.1, bf16[5,384,256]{2,1,0:T(8,128)(2,1)} %kc_hbm.1, bf16[5,384,256]{2,1,0:T(8,128)(2,1)} %vc_hbm.1, s32[5]{0:T(128)} %len_ref.1, bf16[160,256]{1,0:T(8,128)(2,1)} %res_ref.1, ...), custom_call_target="tpu_custom_call" | custom-call | tf_op jit(solution)/shard_map/ffn/pallas_call | solution.py:530
  100.2 1.5 %copy.14 = bf16[160,256]{1,0:T(8,128)(2,1)} copy(bf16[160,256]{1,0:T(8,128)(2,1)} %ffn.1) | data formatting | bytes 163840

commit v4 on v3

--- a/solution.py
+++ b/solution.py
@@ -45,11 +45,11 @@
         self.at, self.sub, self.send, self.recv, self.n = at, sub, send, recv, 0
         self.started = []
 
-    def post(self, src, dst, dim, by):
+    def post(self, src, dst, dim, by, over=0):
         if dim is None:
             to = device(self.at, 1 - self.sub)
         else:
-            to = device(shifted(self.at, dim, by), self.sub)
+            to = device(shifted(shifted(self.at, dim, by), 0, over), self.sub)
         copy = pltpu.make_async_remote_copy(
             src_ref=src, dst_ref=dst, send_sem=self.send.at[self.n], recv_sem=self.recv.at[self.n],
             device_id=to, device_id_type=MESH,
@@ -180,14 +180,23 @@
         ready(step)
     landed(d2d)
     ready(4)
+    late = {}
     for r2, c in ((3, "5"), (1, "3"), (2, "4")):
+        if c == "4":
+            landed(late["5"])
+            ready(5)
+        n = len(d2d)
         for p in range(3):
             for copy in fwd[p, c]:
                 copy.wait_recv()
             across(p, slice(1, 4), r2, 2)
-    landed(d2d[6:])
-    for step in (5, 6, 7, 8):
-        ready(step)
+        late[c] = d2d[n:]
+    landed(late["3"])
+    ready(6)
+    ready(7)
+    landed(late["4"])
+    ready(8)
+    ready(9)
 
 
 def attention(q_ref, nk_ref, nv_ref, kc, vc, len_ref, qs, CB):
@@ -216,7 +225,7 @@
             CB[0, 0, 0, b * 32 + g * 16:b * 32 + (g + 1) * 16] = context.astype(BF16)
 
 
-def project(w, at, sub, CB, LH, wo, wo_load, half_out, half_in, mid_ref):
+def project(w, at, sub, CB, LH, wo, wo_load, half_out, half_in):
     x0, y0, z0 = at
 
     def part(q, rx, ry, rz):
@@ -241,18 +250,16 @@
 
     hop = [w.post(part(q, 0, 0, 0), part(q, 1, 0, 0), 0, 2) for q in range(2)]
     near = [[w.post(cut(q, 0, 0, 0), cut(q, 0, 4 - k, 0), dims[q][0], k) for k in turns] for q in range(2)]
+    far = [[w.post(cut(q, 0, 0, 0), cut(q, 1, 4 - k, 0), dims[q][0], k, over=2) for k in turns] for q in range(2)]
     for q in range(2):
         plane(q, 0, 0)
     settle(0, 0, 0)
-    far = []
-    for q in range(2):
-        hop[q].wait_recv()
-        far.append([w.post(cut(q, 1, 0, 0), cut(q, 1, 4 - k, 0), dims[q][0], k) for k in turns])
     for i in range(3):
         for q in range(2):
             near[q][i].wait_recv()
             plane(q, 0, 4 - turns[i])
     for q in range(2):
+        hop[q].wait_recv()
         plane(q, 1, 0)
     settle(1, 0, 0)
     for i in range(3):
@@ -270,19 +277,14 @@
 
     wo_load.wait()
 
-    def step(i, total):
-        lhs = jnp.concatenate(
-            [LH[pl.ds(pl.multiple_of((i * 8 + j) * ROWS, ROWS), ROWS), :].astype(BF16) for j in range(8)], axis=1
-        )
-        rhs = wo[pl.ds(pl.multiple_of(i * 1024, 1024), 1024), :]
-        return total + jnp.dot(lhs, rhs, preferred_element_type=F32)
-
-    total = lax.fori_loop(0, 4, step, jnp.zeros((ROWS, 512), F32))
-    for core in range(2):
-        half_out[core] = total[:, core * 256:(core + 1) * 256].astype(BF16)
-        mid_ref[core] = total[:, core * 256:(core + 1) * 256]
-    swap = w.post(half_out.at[1 - sub], half_in, None, 0)
-    mine = mid_ref[sub]
+    lhs = jnp.concatenate([LH[h * ROWS:(h + 1) * ROWS, :].astype(BF16) for h in range(32)], axis=1)
+
+    def half(core):
+        return jnp.dot(lhs, wo[:, pl.ds(pl.multiple_of(core * 256, 256), 256)], preferred_element_type=F32)
+
+    half_out[...] = half(1 - sub).astype(BF16)
+    swap = w.post(half_out, half_in, None, 0)
+    mine = half(sub)
     swap.wait_recv()
     return mine + half_in[...].astype(F32)
 
@@ -303,14 +305,18 @@
     for dim in range(3):
         for by in (1, 2, 3):
             pl.semaphore_signal(barrier, inc=1, device_id=device(shifted(at, dim, by), sub), device_id_type=MESH)
+    for dim in (1, 2):
+        for by in (1, 2, 3):
+            to = device(shifted(shifted(at, dim, by), 0, 2), sub)
+            pl.semaphore_signal(barrier, inc=1, device_id=to, device_id_type=MESH)
     pl.semaphore_signal(barrier, inc=1, device_id=device(at, 1 - sub), device_id_type=MESH)
 
     loads[0].wait()
     loads[1].wait()
     attention(q_ref, nk_ref, nv_ref, kc, vc, len_ref, qs, CB)
-    pl.semaphore_wait(barrier, 10)
-    mid = project(w, at, sub, CB, LH, wo, loads[2], half_out, half_in, mid_ref) + res_ref[...].astype(F32)
-    mid_ref[0] = mid
+    pl.semaphore_wait(barrier, 16)
+    mid = project(w, at, sub, CB, LH, wo, loads[2], half_out, half_in) + res_ref[...].astype(F32)
+    mid_ref[...] = mid
     loads = loads[3:]
 
     rows = (mid * gain_ref[...].astype(F32)[None, :]).astype(BF16)
@@ -345,9 +351,9 @@
 
     corner = [(r, 0, rz) for r in (0, 2) for rz in range(4)] + [(r, ry, 0) for r in (0, 2) for ry in (1, 2, 3)]
     odd = [(0, ry, rz) for ry in (1, 3) for rz in (1, 3)]
-    last = [(r, ry, rz) for r in (0, 2) for ry in (1, 2, 3) for rz in (1, 2, 3) if r or ry == 2 or rz == 2]
     batches = {0: corner[0:4], 1: corner[4:8], 2: corner[8:11], 3: corner[11:14], 4: odd,
-               5: last[0:4], 6: last[4:8], 7: last[8:11], 8: last[11:14]}
+               5: [(2, 1, 3), (2, 3, 3), (0, 3, 2)], 6: [(2, 1, 1), (2, 3, 1), (0, 1, 2)], 7: [(0, 2, 1), (0, 2, 3)],
+               8: [(2, 2, 1), (2, 2, 3), (2, 2, 2)], 9: [(2, 1, 2), (2, 3, 2), (0, 2, 2)]}
 
     def ready(step):
         if step == 0:
@@ -380,7 +386,7 @@
         hid[i] = (gate / (1.0 + jnp.exp(-gate)) * up).astype(BF16)
     loads[2].wait()
     scatter(w, dev_at, sub, hid, wd, PB, SB, RB, FB, G1, G3, HB, JB)
-    out_ref[...] = (mid_ref[0] + jnp.concatenate([PB[0, 0, 0, 0], PB[0, 0, 0, 1]], axis=1).astype(F32)).astype(BF16)
+    out_ref[...] = (mid_ref[...] + jnp.concatenate([PB[0, 0, 0, 0], PB[0, 0, 0, 1]], axis=1).astype(F32)).astype(BF16)
     w.drain()
 
 
@@ -501,10 +507,8 @@
             if c == "2":
                 third[p, 0] = [w.post(block(PB, p, 0, k, 0), flat(HB, p, (k - 1, 0)), d2, k) for k in (1, 3, 2)]
 
-    for c in order:
-        pass_on(c)
-    for c in order:
-        collect(c)
+    for kind, c in zip("PPPPPCPCCCCC", "435124035120"):
+        (pass_on if kind == "P" else collect)(c)
     for p in (1, 0, 2):
         d1 = PARTS[p][0][0]
         for k in (2, 1, 3):
@@ -539,9 +543,9 @@
             pltpu.VMEM((ROWS, 128), F32),
             pltpu.VMEM((2, 4, 4, ROWS, 128), BF16),
             pltpu.VMEM((32 * ROWS, 128), F32),
-            pltpu.VMEM((2, ROWS, 256), BF16),
             pltpu.VMEM((ROWS, 256), BF16),
-            pltpu.VMEM((2, ROWS, 256), F32),
+            pltpu.VMEM((ROWS, 256), BF16),
+            pltpu.VMEM((ROWS, 256), F32),
             pltpu.VMEM(grid + (2,) + tail, BF16),
             pltpu.VMEM(grid + tail, BF16),
             pltpu.VMEM((8, 4) + tail, BF16),

time: 102 us -> 101 us (level)
    pallas_call x1, Pallas kernels: 100 us -> 99 us  [ffn(): pl.pallas_call(ffn_kernel, out_shape=jax.ShapeDtypeStruct((ROWS, 256), BF...]
where the time goes in v4:
time: 101 us
  Pallas kernels  99 us (98%)
  local copies, waits for them, and re-layouts  1.53 us (2%)
    pallas_call x1, Pallas kernels, ffn(): pl.pallas_call(ffn_kernel, out_shape=jax.ShapeDtypeStruct((ROWS, 256), BF...  99 us

profile of v4, /device:TPU:0, one launch (start us, length us, event | category | flops | bytes accessed | tf_op | source)
XLA Modules:
  0.0 100.6 jit_solution(6584447467431562766)
XLA Ops:
  0.0 99.0 %ffn.1 = bf16[160,256]{1,0:T(8,128)(2,1)} custom-call(bf16[5,4096]{1,0:T(8,128)(2,1)} %q_ref.1, bf16[5,256]{1,0:T(8,128)(2,1)} %nk_ref.1, bf16[5,256]{1,0:T(8,128)(2,1)} %nv_ref.1, bf16[5,384,256]{2,1,0:T(8,128)(2,1)} %kc_hbm.1, bf16[5,384,256]{2,1,0:T(8,128)(2,1)} %vc_hbm.1, s32[5]{0:T(128)} %len_ref.1, bf16[160,256]{1,0:T(8,128)(2,1)} %res_ref.1, ...), custom_call_target="tpu_custom_call" | custom-call | tf_op jit(solution)/shard_map/ffn/pallas_call | solution.py:534
  99.0 1.5 %copy.14 = bf16[160,256]{1,0:T(8,128)(2,1)} copy(bf16[160,256]{1,0:T(8,128)(2,1)} %ffn.1) | data formatting | bytes 163840
